TPU v7x, 128 devices: a whole 4x4x4 slice. The times are simulated.
128 devices in a mesh: row: 32 (over z, x, core), col: 4 (over y).
Axes of the slice: x: 4, y: 4, z: 4, core: 2. Of those that a mesh axis runs over, the one named last changes fastest.
Arguments:
- noise: float32 [8192, 4096], P('row'), may hold values from -16 to 16
- data: float32 [4096, 4096], P('col', 'row'), may hold values from -16 to 16
Outputs:
- targets: float32 [8192, 4096], P('row', 'col')
- noise_potential: float32 [8192], P('row')
- data_potential: float32 [4096], P('col')
All inputs are finite; a program needn't handle non-finite values.
Results may differ from a plain program's by a relative error of at most 0.0003.
Values sent between devices are 32-bit elements; how exact they have to be, the bound alone decides.
No kernel may reach another device: no remote copies, remote signals or barrier semaphores. Data moves between devices by JAX's collectives and lax.ppermute only.
A program may use at most 128 MiB of HBM per device.

v0:
```python
import math

import jax
import jax.numpy as jnp
from jax import lax
from jax.sharding import PartitionSpec as P

ITERS = 4


EPSILON = 0.02


def row_logsum(scores):
    peak = lax.pmax(jnp.max(scores, axis=1), "col")
    total = lax.psum(jnp.sum(jnp.exp(scores - peak[:, None]), axis=1), "col")
    return peak + jnp.log(total)


def column_logsum(scores):
    peak = lax.pmax(jnp.max(scores, axis=0), "row")
    total = lax.psum(jnp.sum(jnp.exp(scores - peak[None, :]), axis=0), "row")
    return peak + jnp.log(total)


def local(noise, data):
    rows_all = noise.shape[0] * lax.axis_size("row")
    cols_all = data.shape[0] * lax.axis_size("col")
    width = noise.shape[1]
    noise_norm = jnp.sum(noise * noise, axis=1)
    gathered = lax.all_gather(data, "row", axis=1, tiled=True)
    cross = jnp.dot(
        noise, gathered.T, precision=lax.Precision.HIGHEST, preferred_element_type=jnp.float32
    )
    data_norm = jnp.sum(gathered * gathered, axis=1)
    cost = (noise_norm[:, None] + data_norm[None, :] - 2.0 * cross) / width
    data_potential = jnp.zeros((data.shape[0],), jnp.float32)
    for step in range(ITERS):
        noise_potential = -EPSILON * math.log(rows_all) - EPSILON * row_logsum(
            (data_potential[None, :] - cost) / EPSILON
        )
        data_potential = -EPSILON * math.log(cols_all) - EPSILON * column_logsum(
            (noise_potential[:, None] - cost) / EPSILON
        )
    noise_potential = -EPSILON * math.log(rows_all) - EPSILON * row_logsum(
        (data_potential[None, :] - cost) / EPSILON
    )
    weights = (
        jnp.exp((noise_potential[:, None] + data_potential[None, :] - cost) / EPSILON) * rows_all
    )
    partial_targets = jnp.dot(
        weights, gathered, precision=lax.Precision.HIGHEST, preferred_element_type=jnp.float32
    )
    targets = lax.psum_scatter(partial_targets, "col", scatter_dimension=1, tiled=True)
    return (targets, noise_potential, data_potential)


def solution(mesh):
    placed = (P("row", None), P("col", "row"))
    return jax.shard_map(
        local,
        mesh=mesh,
        in_specs=placed,
        out_specs=(P("row", "col"), P("row"), P("col")),
        check_vma=False,
    )
```

profile of v0, /device:TPU:0, one launch (start us, length us, event | category | flops | bytes accessed | tf_op | source)
XLA Modules:
  0.0 780.8 jit_solution(1889171025180773879)
XLA Ops:
  7.2 0.7 all-gather.2.cloned.1.call-update
  7.9 2.6 multiply_reduce_fusion.1
  10.5 83.4 %all-gather.2.cloned.1.call-done = f32[1024,4096]{1,0:T(8,128)} async-done(((f32[1024,128]{1,0:T(8,128)}), f32[1024,4096]{1,0:T(8,128)}) %all-gather.2.cloned.1.call-update) | async-done | bytes 16777232 | tf_op jit(solution)/shard_map/all_gather | solution.py:31
  93.9 6.9 multiply_reduce_fusion
  100.8 17.8 %fusion.8 = (f32[256]{0:T(256)S(1)}, f32[256,1024]{1,0:T(8,128)S(1)}) fusion(f32[256,4096]{1,0:T(8,128)} %param.2, f32[1024,4096]{1,0:T(8,128)} %all-gather.2.cloned.1.call-done, f32[1024]{0:T(1024)S(1)} %multiply_reduce_fusion, f32[256]{0:T(256)S(1)} %multiply_reduce_fusion.1), kind=kOutput, calls=%fused_computation.29 | convolution fusion | flops 12886736896 | bytes 22026240 | tf_op jit(solution)/shard_map/dot_general | solution.py:32
  118.6 10.5 %pmax.63 = f32[256]{0:T(256)S(1)} all-reduce(f32[256]{0:T(256)S(1)} %get-tuple-element.3), channel_id=1, replica_groups=mesh['row'=32,'col'=4] {'col'}, use_global_device_ids=true, to_apply=%region_3.0 | all-reduce | flops 256 | bytes 2048 | tf_op jit(solution)/shard_map/pmax | solution.py:15
  129.1 0.3 exponential_reduce_fusion.8
  129.4 7.7 psum.63
  137.4 62.7 %pmax.64 = f32[1024]{0:T(1024)S(1)} all-reduce(f32[1024]{0:T(1024)S(1)} %fusion.9), channel_id=1, replica_groups=mesh['row'=32,'col'=4] {'row'}, use_global_device_ids=true, to_apply=%region_7.0 | all-reduce | flops 1024 | bytes 8192 | tf_op jit(solution)/shard_map/pmax | solution.py:21
  200.0 0.3 exponential_reduce_fusion.7
  200.3 62.7 %psum.64 = f32[1024]{0:T(1024)S(1)} all-reduce(f32[1024]{0:T(1024)S(1)} %exponential_reduce_fusion.7), channel_id=1, replica_groups=mesh['row'=32,'col'=4] {'row'}, use_global_device_ids=true, to_apply=%region_9.0 | all-reduce | flops 1024 | bytes 8192 | tf_op jit(solution)/shard_map/psum | solution.py:22
  263.2 9.7 %pmax.65 = f32[256]{0:T(256)S(1)} all-reduce(f32[256]{0:T(256)S(1)} %fusion.10), channel_id=1, replica_groups=mesh['row'=32,'col'=4] {'col'}, use_global_device_ids=true, to_apply=%region_11.0 | all-reduce | flops 256 | bytes 2048 | tf_op jit(solution)/shard_map/pmax | solution.py:15
  273.0 0.3 exponential_reduce_fusion.6
  273.3 7.7 psum.65
  281.2 62.7 %pmax.66 = f32[1024]{0:T(1024)S(1)} all-reduce(f32[1024]{0:T(1024)S(1)} %fusion.11), channel_id=1, replica_groups=mesh['row'=32,'col'=4] {'row'}, use_global_device_ids=true, to_apply=%region_15.0 | all-reduce | flops 1024 | bytes 8192 | tf_op jit(solution)/shard_map/pmax | solution.py:21
  343.9 0.3 exponential_reduce_fusion.5
  344.2 62.7 %psum.66 = f32[1024]{0:T(1024)S(1)} all-reduce(f32[1024]{0:T(1024)S(1)} %exponential_reduce_fusion.5), channel_id=1, replica_groups=mesh['row'=32,'col'=4] {'row'}, use_global_device_ids=true, to_apply=%region_17.0 | all-reduce | flops 1024 | bytes 8192 | tf_op jit(solution)/shard_map/psum | solution.py:22
  407.1 9.7 %pmax.67 = f32[256]{0:T(256)S(1)} all-reduce(f32[256]{0:T(256)S(1)} %fusion.12), channel_id=1, replica_groups=mesh['row'=32,'col'=4] {'col'}, use_global_device_ids=true, to_apply=%region_19.0 | all-reduce | flops 256 | bytes 2048 | tf_op jit(solution)/shard_map/pmax | solution.py:15
  416.9 0.3 exponential_reduce_fusion.4
  417.2 7.7 psum.67
  425.1 62.7 %pmax.68 = f32[1024]{0:T(1024)S(1)} all-reduce(f32[1024]{0:T(1024)S(1)} %fusion.13), channel_id=1, replica_groups=mesh['row'=32,'col'=4] {'row'}, use_global_device_ids=true, to_apply=%region_23.0 | all-reduce | flops 1024 | bytes 8192 | tf_op jit(solution)/shard_map/pmax | solution.py:21
  488.1 62.7 %psum.68 = f32[1024]{0:T(1024)S(1)} all-reduce(f32[1024]{0:T(1024)S(1)} %exponential_reduce_fusion.3), channel_id=1, replica_groups=mesh['row'=32,'col'=4] {'row'}, use_global_device_ids=true, to_apply=%region_25.0 | all-reduce | flops 1024 | bytes 8192 | tf_op jit(solution)/shard_map/psum | solution.py:22
  551.0 9.7 %pmax.69 = f32[256]{0:T(256)S(1)} all-reduce(f32[256]{0:T(256)S(1)} %fusion.14), channel_id=1, replica_groups=mesh['row'=32,'col'=4] {'col'}, use_global_device_ids=true, to_apply=%region_27.0 | all-reduce | flops 256 | bytes 2048 | tf_op jit(solution)/shard_map/pmax | solution.py:15
  560.7 0.3 exponential_reduce_fusion.2
  561.1 7.7 psum.69
  569.0 62.7 %pmax.70 = f32[1024]{0:T(1024)S(1)} all-reduce(f32[1024]{0:T(1024)S(1)} %fusion.15), channel_id=1, replica_groups=mesh['row'=32,'col'=4] {'row'}, use_global_device_ids=true, to_apply=%region_31.0 | all-reduce | flops 1024 | bytes 8192 | tf_op jit(solution)/shard_map/pmax | solution.py:21
  632.0 62.7 %psum.70 = f32[1024]{0:T(1024)S(1)} all-reduce(f32[1024]{0:T(1024)S(1)} %exponential_reduce_fusion.1), channel_id=1, replica_groups=mesh['row'=32,'col'=4] {'row'}, use_global_device_ids=true, to_apply=%region_33.0 | all-reduce | flops 1024 | bytes 8192 | tf_op jit(solution)/shard_map/psum | solution.py:22
  694.9 9.7 %pmax.71 = f32[256]{0:T(256)S(1)} all-reduce(f32[256]{0:T(256)S(1)} %fusion.16), channel_id=1, replica_groups=mesh['row'=32,'col'=4] {'col'}, use_global_device_ids=true, to_apply=%region_35.0 | all-reduce | flops 256 | bytes 2048 | tf_op jit(solution)/shard_map/pmax | solution.py:15
  704.6 0.3 exponential_reduce_fusion
  705.0 7.9 %psum.71 = f32[256]{0:T(256)S(1)} all-reduce(f32[256]{0:T(256)S(1)} %exponential_reduce_fusion), channel_id=1, replica_groups=mesh['row'=32,'col'=4] {'col'}, use_global_device_ids=true, to_apply=%region_37.0 | all-reduce | flops 256 | bytes 2048 | tf_op jit(solution)/shard_map/psum | solution.py:16
  712.9 18.7 %fusion.2 = f32[256,4096]{1,0:T(8,128)} fusion(f32[1024,4096]{1,0:T(8,128)} %all-gather.2.cloned.1.call-done, f32[256,1024]{1,0:T(8,128)S(1)} %get-tuple-element.4, f32[256]{0:T(256)S(1)} %multiply_subtract_fusion.4, f32[1024]{0:T(1024)S(1)} %multiply_subtract_fusion), kind=kOutput, calls=%fused_computation.5 | convolution fusion | flops 12885950464 | bytes 22025216 | tf_op jit(solution)/shard_map/dot_general | solution.py:51
  731.7 42.3 %reduce-scatter.2.cloned.1.call-done = f32[256,1024]{1,0:T(8,128)} async-done(((f32[256,4096]{1,0:T(8,128)}), f32[256,1024]{1,0:T(8,128)}) %reduce-scatter.2.cloned.1.call-update) | async-done | bytes 1048592 | tf_op jit(solution)/shard_map/reduce_scatter | solution.py:54
  (26 shorter events, 2.2 us)
Async XLA Ops:
  7.2 86.7 %all-gather.2.cloned.1.call-start = ((), (), s32[]{:S(2)}) async-start(), calls=%async_computation.1 | async-start | bytes 17301504 | tf_op jit(solution)/shard_map/all_gather | solution.py:31
  7.9 766.0 %reduce-scatter.2.cloned.1.call-start = ((), (), s32[]{:S(2)}) async-start(), calls=%async_computation.2 | async-start | bytes 5242880 | tf_op jit(solution)/shard_map/reduce_scatter | solution.py:54
  694.7 79.2 %copy-start = (f32[1024]{0:T(1024)}, f32[1024]{0:T(1024)S(1)}, u32[]{:S(2)}) copy-start(f32[1024]{0:T(1024)S(1)} %multiply_subtract_fusion) | copy-start | bytes 12292
  712.9 61.0 %copy-start.1 = (f32[256]{0:T(256)}, f32[256]{0:T(256)S(1)}, u32[]{:S(2)}) copy-start(f32[256]{0:T(256)S(1)} %multiply_subtract_fusion.4) | copy-start | bytes 3076
Sparse Core Ops, SparseCore 0:
  10.2 83.6 all-gather.1
  731.8 42.0 reduce-scatter.1
where the time goes:
time: 782 us; the launch traced here: 781 us
  blocking collectives  590 us (75%)
  waiting for transfers between devices  126 us (16%)
  matrix products  36.5 us (5%)
  between operations  14.1 us (2%)
  other arithmetic  13.9 us (2%)
    psum x4, blocking collectives, column_logsum(): total = lax.psum(jnp.sum(jnp.exp(scores - peak[None, :]), axis=0), 'row')  251 us
    pmax x4, blocking collectives, column_logsum(): peak = lax.pmax(jnp.max(scores, axis=0), 'row')  251 us
    all_gather x1, waiting for transfers between devices, local(): gathered = lax.all_gather(data, 'row', axis=1, tiled=True)  83.4 us
    pmax x5, blocking collectives, row_logsum(): peak = lax.pmax(jnp.max(scores, axis=1), 'col')  49.5 us
    reduce_scatter x1, waiting for transfers between devices, local(): lax.psum_scatter(partial_targets, 'col', scatter_dimension=1, tiled=True)  42.3 us
    psum x5, blocking collectives, row_logsum(): total = lax.psum(jnp.sum(jnp.exp(scores - peak[:, None]), axis=1), 'col')  38.9 us
    dot_general x1, matrix products, local(): jnp.dot(weights, gathered, precision=lax.Precision.HIGHEST, preferred_ele...  18.7 us
    dot_general x1, matrix products, local(): jnp.dot(noise, gathered.T, precision=lax.Precision.HIGHEST, preferred_ele...  17.8 us
  transfers between devices with their start and end apart: 2, of which 2 were waited for; matrix products, arithmetic and copies ran while one was open for 0% of the time, Pallas kernels for 0%

commit v1 on v0

v1 whole, which is shorter than its diff:
```python
import functools
import math

import jax
import jax.numpy as jnp
from jax import lax
from jax.experimental import pallas as pl
from jax.experimental.pallas import tpu as pltpu
from jax.sharding import PartitionSpec as P

ITERS = 4
EPSILON = 0.02
LOG2E = 1.0 / math.log(2.0)
SCALE = LOG2E / EPSILON
VMEM_LIMIT = 48 * 1024 * 1024


def split(v):
    hi = v.astype(jnp.bfloat16)
    return hi, (v - hi.astype(jnp.float32)).astype(jnp.bfloat16)


def dot3(a, b, dims):
    a_hi, a_lo = split(a)
    b_hi, b_lo = split(b)
    mul = functools.partial(
        lax.dot_general, dimension_numbers=(dims, ((), ())), preferred_element_type=jnp.float32
    )
    return mul(a_hi, b_hi) + (mul(a_hi, b_lo) + mul(a_lo, b_hi))


def cross_kernel(factor, noise_ref, data_ref, cross_ref, norm_ref, square_ref):
    step = pl.program_id(0)
    joined = jnp.concatenate([data_ref[0], data_ref[1]], axis=1)
    columns = pl.ds(pl.multiple_of(step * joined.shape[1], joined.shape[1]), joined.shape[1])
    product = dot3(noise_ref[:, columns], joined, ((1,), (1,)))
    squares = data_ref[0] * data_ref[0] + data_ref[1] * data_ref[1]

    @pl.when(step == 0)
    def _():
        cross_ref[...] = product
        square_ref[...] = squares

    @pl.when(step > 0)
    def _():
        cross_ref[...] += product
        square_ref[...] += squares

    @pl.when(step == pl.num_programs(0) - 1)
    def _():
        cross_ref[...] = cross_ref[...] * factor
        norm_ref[...] = lax.dot_general(
            jnp.ones((8, square_ref.shape[1]), jnp.float32),
            square_ref[...],
            (((1,), (1,)), ((), ())),
            precision=lax.Precision.HIGHEST,
            preferred_element_type=jnp.float32,
        )


def cross_products(noise, gathered):
    rows, width = noise.shape
    blocks, cols, part = gathered.shape
    return pl.pallas_call(
        functools.partial(cross_kernel, 2.0 * SCALE / width),
        grid=(blocks // 2,),
        in_specs=[
            pl.BlockSpec((rows, width), lambda s: (0, 0)),
            pl.BlockSpec((2, cols, part), lambda s: (s, 0, 0)),
        ],
        out_specs=[
            pl.BlockSpec((rows, cols), lambda s: (0, 0)),
            pl.BlockSpec((8, cols), lambda s: (0, 0)),
        ],
        out_shape=[
            jax.ShapeDtypeStruct((rows, cols), jnp.float32),
            jax.ShapeDtypeStruct((8, cols), jnp.float32),
        ],
        scratch_shapes=[pltpu.VMEM((cols, part), jnp.float32)],
        compiler_params=pltpu.CompilerParams(vmem_limit_bytes=VMEM_LIMIT),
        cost_estimate=pl.CostEstimate(
            flops=6 * rows * cols * width, bytes_accessed=4 * cols * width, transcendentals=0
        ),
    )(noise, gathered)


def target_kernel(
    place_ref,
    noise_ref,
    data_pot_ref,
    own_ref,
    left0_ref,
    left1_ref,
    right0_ref,
    right1_ref,
    far0_ref,
    far1_ref,
    data_ref,
    target_ref,
    total_ref,
    sums_ref,
):
    offset, quarter = pl.program_id(0), pl.program_id(1)
    depth = data_ref.shape[3]
    half = left0_ref.shape[0]
    peer = lax.rem(place_ref[0] + 4 - offset, 4)
    columns = pl.ds(pl.multiple_of(quarter * depth, depth), depth)
    values = jnp.concatenate([data_ref[0, b, 0] for b in range(data_ref.shape[1])], axis=1)
    data_hi, data_lo = split(values)

    @pl.when((offset == 0) & (quarter == 0))
    def _():
        target_ref[...] = jnp.zeros_like(target_ref)
        sums_ref[...] = jnp.zeros_like(sums_ref)

    def accumulate(refs):
        for part, ref in enumerate(refs):
            height = ref.shape[0]
            rows = pl.ds(part * height, height)
            score = ref[:, columns] + noise_ref[rows, :] + data_pot_ref[offset, :, columns]
            weight = jnp.exp2(score)
            folded = sum(weight[:, c : c + 128] for c in range(0, depth, 128))
            sums_ref[peer, rows, :] += folded
            w_hi, w_lo = split(weight)
            mul = functools.partial(jnp.dot, preferred_element_type=jnp.float32)
            target_ref[rows, :] += mul(w_hi, data_hi) + (mul(w_hi, data_lo) + mul(w_lo, data_hi))

    pieces = ((own_ref,), (left0_ref, left1_ref), (far0_ref, far1_ref), (right0_ref, right1_ref))
    for which, refs in enumerate(pieces):
        pl.when(offset == which)(functools.partial(accumulate, refs))

    @pl.when((offset == 3) & (quarter == 3))
    def _():
        total = (sums_ref[0] + sums_ref[1]) + (sums_ref[2] + sums_ref[3])
        total = jnp.sum(total, axis=1, keepdims=True)
        target_ref[...] = target_ref[...] / total
        total_ref[...] = jnp.broadcast_to(total, total_ref.shape)


def weighted_targets(place, noise_pot, data_pots, own, left, right, far, gathered):
    rows, cols = own.shape
    part = gathered.shape[-1]
    data = gathered.reshape(4, 8, 4, cols // 4, part)
    whole = lambda shape: pl.BlockSpec(shape, lambda o, q, place: (0,) * len(shape))
    half = (rows // 2, cols)
    return pl.pallas_call(
        target_kernel,
        grid_spec=pltpu.PrefetchScalarGridSpec(
            num_scalar_prefetch=1,
            grid=(4, 4),
            in_specs=[
                whole((rows, 1)),
                whole((4, 1, cols)),
                whole((rows, cols)),
                *[whole(half)] * 6,
                pl.BlockSpec(
                    (1, 8, 1, cols // 4, part),
                    lambda o, q, place: (q, 0, lax.rem(q + 4 - place[0] + o, 4), 0, 0),
                ),
            ],
            out_specs=[whole((rows, 8 * part)), whole((rows, 128))],
            scratch_shapes=[pltpu.VMEM((4, rows, 128), jnp.float32)],
        ),
        out_shape=[
            jax.ShapeDtypeStruct((rows, 8 * part), jnp.float32),
            jax.ShapeDtypeStruct((rows, 128), jnp.float32),
        ],
        compiler_params=pltpu.CompilerParams(vmem_limit_bytes=VMEM_LIMIT),
        cost_estimate=pl.CostEstimate(
            flops=24 * rows * cols * 8 * part, bytes_accessed=20 * 1024 * 1024, transcendentals=4 * rows * cols
        ),
    )(place, noise_pot, data_pots, own, *left, *right, *far, data)


def shift(v, by):
    return lax.ppermute(v, "col", [(i, (i + by) % 4) for i in range(4)])


def around(v):
    return shift(v, 1), shift(v, 2), shift(v, 3)


def spread(v):
    return lax.all_to_all(jnp.broadcast_to(v[None], (32,) + v.shape), "row", 0, 0, tiled=True)


def pair_logsum(peaks, totals):
    peak = functools.reduce(jnp.maximum, peaks)
    scaled = [t * jnp.exp2(p - peak) for p, t in zip(peaks, totals)]
    return peak + jnp.log2((scaled[0] + scaled[2]) + (scaled[1] + scaled[3]))


def local(noise, data):
    rows, width = noise.shape
    cols, part = data.shape
    rows_all, cols_all = rows * 32, cols * 4
    log_rows, log_cols = math.log2(rows_all), math.log2(cols_all)
    place = lax.axis_index("col")
    quarter = cols // 4

    pieces = []
    for k in range(4):
        block = lax.dynamic_slice(data, (lax.rem(place + k, 4) * quarter, 0), (quarter, part))
        pairs = []
        for z in range(4):
            for xc in range(8):
                for y in range(4):
                    pairs.append(((z * 8 + xc) * 4 + y, (((y + k) % 4) * 8 + xc) * 4 + z))
        pieces.append(lax.ppermute(block, ("row", "col"), pairs))
    turned = jnp.concatenate(pieces, axis=0)

    gathered = lax.all_gather(data, "row", axis=0, tiled=False)
    noise_norm = jnp.sum(noise * noise, axis=1) / width
    scores, norms = cross_products(noise, gathered)
    data_norm = norms[0] / width

    gathered, turned = lax.optimization_barrier((gathered, turned))
    turned = lax.all_gather(turned, "row", axis=0, tiled=False)

    shifted = scores - (data_norm * SCALE)[None, :]
    peak = jnp.max(shifted, axis=1)
    total = jnp.sum(jnp.exp2(shifted - peak[:, None]), axis=1)
    pair = jnp.stack([peak, total])
    pairs = (pair,) + around(pair)
    noise_pot = -log_rows - pair_logsum([p[0] for p in pairs], [p[1] for p in pairs])

    halves = (scores[: rows // 2], scores[rows // 2 :])
    shifted = scores + noise_pot[:, None]
    peak = jnp.max(shifted, axis=0)
    total = jnp.sum(jnp.exp2(shifted - peak[None, :]), axis=0)
    pair = jnp.concatenate([peak, total]).reshape(16, 128)
    pair, first = lax.optimization_barrier((pair, halves[0]))
    left0, right0 = shift(first, 1), shift(first, 3)
    pairs = spread(pair)
    pairs, left0, right0 = lax.optimization_barrier((pairs, left0, right0))
    peaks, totals = pairs[:, :8].reshape(32, cols), pairs[:, 8:].reshape(32, cols)
    peak = jnp.max(peaks, axis=0)
    total = jnp.sum(totals * jnp.exp2(peaks - peak[None, :]), axis=0)
    data_pot = -log_cols - (peak + jnp.log2(total))

    for step in range(1, ITERS):
        total = jnp.sum(jnp.exp2(scores + noise_pot[:, None] + data_pot[None, :]), axis=1)
        one, two, three = around(total)
        noise_pot = noise_pot - log_rows - jnp.log2((total + two) + (one + three))
        total = jnp.sum(jnp.exp2(scores + noise_pot[:, None] + data_pot[None, :]), axis=0)
        total = total.reshape(8, 128)
        if step == 1:
            total, second = lax.optimization_barrier((total, halves[1]))
            left1, right1 = shift(second, 1), shift(second, 3)
            totals = spread(total)
            totals, left1, right1 = lax.optimization_barrier((totals, left1, right1))
        elif step == 2:
            total, left0, right1 = lax.optimization_barrier((total, left0, right1))
            far0, far1 = shift(left0, 1), shift(right1, 3)
            totals = spread(total)
            totals, far0, far1 = lax.optimization_barrier((totals, far0, far1))
        else:
            totals = spread(total)
        data_pot = data_pot - log_cols - jnp.log2(jnp.sum(totals, axis=0).reshape(cols))

    data_pots = jnp.stack((data_pot,) + around(data_pot))[:, None, :]
    targets, total = weighted_targets(
        place.reshape(1).astype(jnp.int32),
        noise_pot[:, None],
        data_pots,
        scores,
        (left0, left1),
        (right0, right1),
        (far0, far1),
        turned,
    )
    noise_pot = noise_pot - log_rows - jnp.log2(total[:, 0])
    return (targets, noise_norm + noise_pot / SCALE, data_norm + data_pot / SCALE)


def solution(mesh):
    placed = (P("row", None), P("col", "row"))
    return jax.shard_map(
        local,
        mesh=mesh,
        in_specs=placed,
        out_specs=(P("row", "col"), P("row"), P("col")),
        check_vma=False,
    )
```

time: 782 us -> 251 us (0.32)
  blocking collectives: 590 us -> 40.9 us
  starting transfers between devices: 0.08 us -> 50.1 us
  Pallas kernels: 0 us -> 37.5 us
  matrix products: 36.5 us -> 0 us
  waiting for transfers between devices: 126 us -> 90.7 us
  local copies, waits for them, and re-layouts: 0.01 us -> 7.91 us
    pmax x9 -> x0, blocking collectives: 300 us -> none  [the longest x4 251 us: column_logsum(): peak = lax.pmax(jnp.max(scores, axis=0), 'row')]
    psum x9 -> x0, blocking collectives: 290 us -> none  [the longest x4 251 us: column_logsum(): total = lax.psum(jnp.sum(jnp.exp(scores - peak[None, :]), axis=0), 'row')]
    ppermute x0 -> x25, starting transfers between devices: none -> 46.2 us  [the longest x21 33.5 us: shift(): return lax.ppermute(v, 'col', [(i, (i + by) % 4) for i in range(4)])]
    reduce_scatter x1 -> x0, waiting for transfers between devices: 42.3 us -> none  [local(): lax.psum_scatter(partial_targets, 'col', scatter_dimension=1, tiled=True)]
    all_to_all x0 -> x3, blocking collectives: none -> 40.9 us  [spread(): lax.all_to_all(jnp.broadcast_to(v[None], (32,) + v.shape), 'row', 0, 0, t...]
    pallas_call x0 -> x2, Pallas kernels: none -> 37.5 us  [the longest x1 19.6 us: weighted_targets(): pl.pallas_call(target_kernel, grid_spec=pltpu.PrefetchScalarGridSpec(num_...]
    dot_general x2 -> x0, matrix products: 36.5 us -> none  [the longest x1 18.7 us: local(): jnp.dot(weights, gathered, precision=lax.Precision.HIGHEST, preferred_ele...]
    ppermute x0 -> x25, waiting for transfers between devices: none -> 30.1 us  [the longest x4 18.5 us: local(): pieces.append(lax.ppermute(block, ('row', 'col'), pairs))]
  transfers between devices with their start and end apart: 2 -> 28, of which waited for: 2 -> 18; matrix products, arithmetic and copies ran while one was open for 0% -> 4% of each run, Pallas kernels for 0% -> 7%
where the time goes in v1:
time: 251 us; the launch traced here: 249 us
  waiting for transfers between devices  90.7 us (36%)
  starting transfers between devices  50.1 us (20%)
  blocking collectives  40.9 us (16%)
  Pallas kernels  37.5 us (15%)
  between operations  14.3 us (6%)
  other arithmetic  7.99 us (3%)
  local copies, waits for them, and re-layouts  7.91 us (3%)
    all_gather x1, waiting for transfers between devices, local(): gathered = lax.all_gather(data, 'row', axis=0, tiled=False)  54.8 us
    all_to_all x3, blocking collectives, spread(): lax.all_to_all(jnp.broadcast_to(v[None], (32,) + v.shape), 'row', 0, 0, t...  40.9 us
    ppermute x21, starting transfers between devices, shift(): return lax.ppermute(v, 'col', [(i, (i + by) % 4) for i in range(4)])  33.5 us
    pallas_call x1, Pallas kernels, weighted_targets(): pl.pallas_call(target_kernel, grid_spec=pltpu.PrefetchScalarGridSpec(num_...  19.6 us
    ppermute x4, waiting for transfers between devices, local(): pieces.append(lax.ppermute(block, ('row', 'col'), pairs))  18.5 us
    pallas_call x1, Pallas kernels, cross_products(): pl.pallas_call(functools.partial(cross_kernel, 2.0 * SCALE / width), grid...  18 us
    ppermute x4, starting transfers between devices, local(): pieces.append(lax.ppermute(block, ('row', 'col'), pairs))  12.8 us
    ppermute x21, waiting for transfers between devices, shift(): return lax.ppermute(v, 'col', [(i, (i + by) % 4) for i in range(4)])  11.6 us
  transfers between devices with their start and end apart: 28, of which 18 were waited for; matrix products, arithmetic and copies ran while one was open for 4% of the time, Pallas kernels for 7%

profile of v1, /device:TPU:0, one launch (start us, length us, event | category | flops | bytes accessed | tf_op | source)
XLA Modules:
  0.0 249.4 jit_solution(9884795482015667315)
XLA Ops:
  9.8 4.4 %collective-permute-start.22 = (f32[256,128]{1,0:T(8,128)S(1)}, f32[256,128]{1,0:T(8,128)S(1)}, u32[]{:S(2)}, u32[]{:S(2)}) collective-permute-start(f32[256,128]{1,0:T(8,128)S(1)} %get-tuple-element.52), channel_id=1, source_target_pairs={{0,32},{1,64},{2,96},{3,0},{4,36},{5,68},{6,100},{7,4},{8,40},{9,7... | collective-permute-start | bytes 393224 | tf_op jit(solution)/shard_map/ppermute | solution.py:209
  14.2 5.4 %collective-permute-start.23 = (f32[256,128]{1,0:T(8,128)S(1)}, f32[256,128]{1,0:T(8,128)S(1)}, u32[]{:S(2)}, u32[]{:S(2)}) collective-permute-start(f32[256,128]{1,0:T(8,128)S(1)} %get-tuple-element.54), channel_id=1, source_target_pairs={{0,64},{1,96},{2,0},{3,32},{4,68},{5,100},{6,4},{7,36},{8,72},{9,1... | collective-permute-start | bytes 393224 | tf_op jit(solution)/shard_map/ppermute | solution.py:209
  19.6 2.3 collective-permute-start.24
  21.9 13.5 %collective-permute-done.22 = f32[256,128]{1,0:T(8,128)S(1)} collective-permute-done((f32[256,128]{1,0:T(8,128)S(1)}, f32[256,128]{1,0:T(8,128)S(1)}, u32[]{:S(2)}, u32[]{:S(2)}) %collective-permute-start.22) | collective-permute-done | bytes 131104 | tf_op jit(solution)/shard_map/ppermute | solution.py:209
  35.3 5.0 %collective-permute-done.23 = f32[256,128]{1,0:T(8,128)S(1)} collective-permute-done((f32[256,128]{1,0:T(8,128)S(1)}, f32[256,128]{1,0:T(8,128)S(1)}, u32[]{:S(2)}, u32[]{:S(2)}) %collective-permute-start.23) | collective-permute-done | bytes 131104 | tf_op jit(solution)/shard_map/ppermute | solution.py:209
  41.2 54.8 %all-gather.5.cloned.1.call-done = f32[32768,128]{1,0:T(8,128)} async-done(((f32[1024,128]{1,0:T(8,128)}), f32[32768,128]{1,0:T(8,128)}) %all-gather.5.cloned.1.call-update) | async-done | bytes 16777232 | tf_op jit(solution)/shard_map/all_gather | solution.py:212
  96.0 2.2 copy-done
  98.2 18.0 %shard_map.49 = (f32[256,1024]{1,0:T(8,128)S(1)}, f32[8,1024]{1,0:T(8,128)S(1)}) custom-call(f32[256,4096]{1,0:T(8,128)S(1)} %copy-done, f32[32,1024,128]{2,1,0:T(8,128)} %bitcast.56), custom_call_target="tpu_custom_call" | custom-call | flops 6442450944 | bytes 16777216 | tf_op jit(solution)/shard_map/pallas_call | solution.py:64
  116.7 2.8 %collective-permute-start.2 = (f32[2,256]{1,0:T(2,128)S(1)}, f32[2,256]{1,0:T(2,128)S(1)}, u32[]{:S(2)}, u32[]{:S(2)}) collective-permute-start(f32[2,256]{1,0:T(2,128)S(1)} %pad_maximum_fusion.3), channel_id=1, source_target_pairs={{0,3},{1,0},{2,1},{3,2},{4,7},{5,4},{6,5},{7,6},{8,11},{9,8},{10,9... | collective-permute-start | bytes 6152 | tf_op jit(solution)/shard_map/ppermute | solution.py:176
  119.6 2.3 collective-permute-start.1
  121.9 2.4 collective-permute-done
  126.0 2.6 %collective-permute-start.4 = (f32[128,1024]{1,0:T(8,128)S(1)}, f32[128,1024]{1,0:T(8,128)S(1)}, u32[]{:S(2)}, u32[]{:S(2)}) collective-permute-start(f32[128,1024]{1,0:T(8,128)S(1)} %get-tuple-element.27), channel_id=1, source_target_pairs={{0,3},{1,0},{2,1},{3,2},{4,7},{5,4},{6,5},{7,6},{8,11},{9,8},{10,9... | collective-permute-start | bytes 1572872 | tf_op jit(solution)/shard_map/ppermute | solution.py:176
  128.5 17.1 %all_to_all.20 = f32[32,16,128]{2,1,0:T(8,128)S(1)} all-to-all(f32[32,16,128]{2,1,0:T(8,128)S(1)} %broadcast_in_dim.14), channel_id=1, replica_groups=mesh['row'=32,'col'=4] {'row'}, dimensions={0} | all-to-all | bytes 524288 | tf_op jit(solution)/shard_map/all_to_all | solution.py:184
  146.2 1.4 collective-permute-start.5
  147.6 1.5 collective-permute-start.6
  149.0 1.8 collective-permute-start.7
  153.7 2.6 %collective-permute-start.9 = (f32[128,1024]{1,0:T(8,128)S(1)}, f32[128,1024]{1,0:T(8,128)S(1)}, u32[]{:S(2)}, u32[]{:S(2)}) collective-permute-start(f32[128,1024]{1,0:T(8,128)S(1)} %get-tuple-element.30), channel_id=1, source_target_pairs={{0,3},{1,0},{2,1},{3,2},{4,7},{5,4},{6,5},{7,6},{8,11},{9,8},{10,9... | collective-permute-start | bytes 1572872 | tf_op jit(solution)/shard_map/ppermute | solution.py:176
  156.2 12.4 %all_to_all.21 = f32[32,8,128]{2,1,0:T(8,128)S(1)} all-to-all(f32[32,8,128]{2,1,0:T(8,128)S(1)} %broadcast_in_dim.15), channel_id=1, replica_groups=mesh['row'=32,'col'=4] {'row'}, dimensions={0} | all-to-all | bytes 262144 | tf_op jit(solution)/shard_map/all_to_all | solution.py:184
  170.3 1.4 collective-permute-start.11
  171.7 1.8 collective-permute-start.12
  176.6 2.4 collective-permute-start.14
  178.9 11.4 %all_to_all.22 = f32[32,8,128]{2,1,0:T(8,128)S(1)} all-to-all(f32[32,8,128]{2,1,0:T(8,128)S(1)} %broadcast_in_dim.16), channel_id=1, replica_groups=mesh['row'=32,'col'=4] {'row'}, dimensions={0} | all-to-all | bytes 262144 | tf_op jit(solution)/shard_map/all_to_all | solution.py:184
  192.3 1.5 collective-permute-start.15
  193.8 1.4 collective-permute-start.16
  195.2 1.8 collective-permute-start.17
  199.8 3.8 %all-to-all-start.3 = ((f32[32,8,128]{2,1,0:T(8,128)}), f32[32,8,128]{2,1,0:T(8,128)S(1)}, u32[]{:S(2)}, u32[]{:S(2)}) async-start(f32[32,8,128]{2,1,0:T(8,128)} %broadcast_in_dim.19), calls=%async_computation.3 | async-start | bytes 262144 | tf_op jit(solution)/shard_map/all_to_all | solution.py:184
  203.6 2.6 %multiply_reduce_fusion = f32[256]{0:T(256)S(1)} fusion(f32[256,4096]{1,0:T(8,128)} %noise_ref.1), kind=kLoop, calls=%fused_computation | loop fusion | flops 2096896 | bytes 4195328 | tf_op jit(solution)/shard_map/reduce_sum | solution.py:213
  206.3 5.1 %all-to-all-done.3 = f32[32,8,128]{2,1,0:T(8,128)S(1)} async-done(((f32[32,8,128]{2,1,0:T(8,128)}), f32[32,8,128]{2,1,0:T(8,128)S(1)}, u32[]{:S(2)}, u32[]{:S(2)}) %all-to-all-start.3) | async-done | bytes 131104 | tf_op jit(solution)/shard_map/all_to_all | solution.py:184
  212.8 3.8 %collective-permute-start.19 = (f32[1024]{0:T(1024)S(1)}, f32[1024]{0:T(1024)S(1)}, u32[]{:S(2)}, u32[]{:S(2)}) collective-permute-start(f32[1024]{0:T(1024)S(1)} %get-tuple-element.46), channel_id=1, source_target_pairs={{0,2},{1,3},{2,0},{3,1},{4,6},{5,7},{6,4},{7,5},{8,10},{9,11},{10,... | collective-permute-start | bytes 12296 | tf_op jit(solution)/shard_map/ppermute | solution.py:176
  216.9 1.3 collective-permute-done.19
  218.2 2.0 collective-permute-done.20
  222.3 19.6 %shard_map.50 = (f32[256,1024]{1,0:T(8,128)}, f32[256,128]{1,0:T(8,128)S(1)}) custom-call(s32[1]{0:T(128)} %bitcast.place_ref, f32[256,1]{1,0:T(8,128)S(1)} %copy.6.noise_ref, f32[4,1,1024]{2,1,0:T(1,128)S(1)} %broadcast_in_dim.20.data_pot_ref, f32[256,1024]{1,0:T(8,128)S(1)} %get-tuple-element.24.own_ref, f32[128,1024]{1,0:T(8,128)S(1)} %collective-permute-done.3.left0_ref, ...), custom_call_target="tpu_custom_call" | custom-call | flops 6442450944 | bytes 20971520 | tf_op jit(solution)/shard_map/pallas_call | solution.py:146
  (84 shorter events, 23.1 us)
Async XLA Ops:
  7.2 88.8 %all-gather.5.cloned.1.call-start = ((), (), s32[]{:S(2)}) async-start(), calls=%async_computation.4 | async-start | bytes 17301504 | tf_op jit(solution)/shard_map/all_gather | solution.py:212
  7.9 212.3 %all-gather.7.cloned.1.call-start = ((), (), s32[]{:S(2)}) async-start(), calls=%async_computation.5 | async-start | bytes 17301504 | tf_op jit(solution)/shard_map/all_gather | solution.py:218
  9.1 12.8 %collective-permute-start.21 = (f32[256,128]{1,0:T(8,128)S(1)}, f32[256,128]{1,0:T(8,128)S(1)}, u32[]{:S(2)}, u32[]{:S(2)}) collective-permute-start(f32[256,128]{1,0:T(8,128)S(1)} %get-tuple-element.51), channel_id=1, source_target_pairs={{0,0},{1,32},{2,64},{3,96},{4,4},{5,36},{6,68},{7,100},{8,8},{9,40... | collective-permute-start | bytes 393224 | tf_op jit(solution)/shard_map/ppermute | solution.py:209
  9.8 25.5 %collective-permute-start.22 = (f32[256,128]{1,0:T(8,128)S(1)}, f32[256,128]{1,0:T(8,128)S(1)}, u32[]{:S(2)}, u32[]{:S(2)}) collective-permute-start(f32[256,128]{1,0:T(8,128)S(1)} %get-tuple-element.52), channel_id=1, source_target_pairs={{0,32},{1,64},{2,96},{3,0},{4,36},{5,68},{6,100},{7,4},{8,40},{9,7... | collective-permute-start | bytes 393224 | tf_op jit(solution)/shard_map/ppermute | solution.py:209
  14.2 26.1 %collective-permute-start.23 = (f32[256,128]{1,0:T(8,128)S(1)}, f32[256,128]{1,0:T(8,128)S(1)}, u32[]{:S(2)}, u32[]{:S(2)}) collective-permute-start(f32[256,128]{1,0:T(8,128)S(1)} %get-tuple-element.54), channel_id=1, source_target_pairs={{0,64},{1,96},{2,0},{3,32},{4,68},{5,100},{6,4},{7,36},{8,72},{9,1... | collective-permute-start | bytes 393224 | tf_op jit(solution)/shard_map/ppermute | solution.py:209
  19.6 20.8 %collective-permute-start.24 = (f32[256,128]{1,0:T(8,128)S(1)}, f32[256,128]{1,0:T(8,128)S(1)}, u32[]{:S(2)}, u32[]{:S(2)}) collective-permute-start(f32[256,128]{1,0:T(8,128)S(1)} %get-tuple-element.53), channel_id=1, source_target_pairs={{0,96},{1,0},{2,32},{3,64},{4,100},{5,4},{6,36},{7,68},{8,104},{9,... | collective-permute-start | bytes 393224 | tf_op jit(solution)/shard_map/ppermute | solution.py:209
  96.0 2.2 copy-start
  116.7 5.2 %collective-permute-start.2 = (f32[2,256]{1,0:T(2,128)S(1)}, f32[2,256]{1,0:T(2,128)S(1)}, u32[]{:S(2)}, u32[]{:S(2)}) collective-permute-start(f32[2,256]{1,0:T(2,128)S(1)} %pad_maximum_fusion.3), channel_id=1, source_target_pairs={{0,3},{1,0},{2,1},{3,2},{4,7},{5,4},{6,5},{7,6},{8,11},{9,8},{10,9... | collective-permute-start | bytes 6152 | tf_op jit(solution)/shard_map/ppermute | solution.py:176
  119.6 4.8 %collective-permute-start = (f32[2,256]{1,0:T(2,128)S(1)}, f32[2,256]{1,0:T(2,128)S(1)}, u32[]{:S(2)}, u32[]{:S(2)}) collective-permute-start(f32[2,256]{1,0:T(2,128)S(1)} %pad_maximum_fusion.3), channel_id=1, source_target_pairs={{0,1},{1,2},{2,3},{3,0},{4,5},{5,6},{6,7},{7,4},{8,9},{9,10},{10,1... | collective-permute-start | bytes 6152 | tf_op jit(solution)/shard_map/ppermute | solution.py:176
  119.6 5.1 %collective-permute-start.1 = (f32[2,256]{1,0:T(2,128)S(1)}, f32[2,256]{1,0:T(2,128)S(1)}, u32[]{:S(2)}, u32[]{:S(2)}) collective-permute-start(f32[2,256]{1,0:T(2,128)S(1)} %pad_maximum_fusion.3), channel_id=1, source_target_pairs={{0,2},{1,3},{2,0},{3,1},{4,6},{5,7},{6,4},{7,5},{8,10},{9,11},{10,... | collective-permute-start | bytes 6152 | tf_op jit(solution)/shard_map/ppermute | solution.py:176
  125.1 20.5 %collective-permute-start.3 = (f32[128,1024]{1,0:T(8,128)S(1)}, f32[128,1024]{1,0:T(8,128)S(1)}, u32[]{:S(2)}, u32[]{:S(2)}) collective-permute-start(f32[128,1024]{1,0:T(8,128)S(1)} %get-tuple-element.27), channel_id=1, source_target_pairs={{0,1},{1,2},{2,3},{3,0},{4,5},{5,6},{6,7},{7,4},{8,9},{9,10},{10,1... | collective-permute-start | bytes 1572872 | tf_op jit(solution)/shard_map/ppermute | solution.py:176
  126.0 19.7 %collective-permute-start.4 = (f32[128,1024]{1,0:T(8,128)S(1)}, f32[128,1024]{1,0:T(8,128)S(1)}, u32[]{:S(2)}, u32[]{:S(2)}) collective-permute-start(f32[128,1024]{1,0:T(8,128)S(1)} %get-tuple-element.27), channel_id=1, source_target_pairs={{0,3},{1,0},{2,1},{3,2},{4,7},{5,4},{6,5},{7,6},{8,11},{9,8},{10,9... | collective-permute-start | bytes 1572872 | tf_op jit(solution)/shard_map/ppermute | solution.py:176
  146.2 5.2 %collective-permute-start.5 = (f32[256]{0:T(256)S(1)}, f32[256]{0:T(256)S(1)}, u32[]{:S(2)}, u32[]{:S(2)}) collective-permute-start(f32[256]{0:T(256)S(1)} %exponential_reduce_fusion.5), channel_id=1, source_target_pairs={{0,2},{1,3},{2,0},{3,1},{4,6},{5,7},{6,4},{7,5},{8,10},{9,11},{10,... | collective-permute-start | bytes 3080 | tf_op jit(solution)/shard_map/ppermute | solution.py:176
  147.6 4.8 %collective-permute-start.6 = (f32[256]{0:T(256)S(1)}, f32[256]{0:T(256)S(1)}, u32[]{:S(2)}, u32[]{:S(2)}) collective-permute-start(f32[256]{0:T(256)S(1)} %exponential_reduce_fusion.5), channel_id=1, source_target_pairs={{0,1},{1,2},{2,3},{3,0},{4,5},{5,6},{6,7},{7,4},{8,9},{9,10},{10,1... | collective-permute-start | bytes 3080 | tf_op jit(solution)/shard_map/ppermute | solution.py:176
  149.0 3.6 %collective-permute-start.7 = (f32[256]{0:T(256)S(1)}, f32[256]{0:T(256)S(1)}, u32[]{:S(2)}, u32[]{:S(2)}) collective-permute-start(f32[256]{0:T(256)S(1)} %exponential_reduce_fusion.5), channel_id=1, source_target_pairs={{0,3},{1,0},{2,1},{3,2},{4,7},{5,4},{6,5},{7,6},{8,11},{9,8},{10,9... | collective-permute-start | bytes 3080 | tf_op jit(solution)/shard_map/ppermute | solution.py:176
  152.9 15.7 %collective-permute-start.8 = (f32[128,1024]{1,0:T(8,128)S(1)}, f32[128,1024]{1,0:T(8,128)S(1)}, u32[]{:S(2)}, u32[]{:S(2)}) collective-permute-start(f32[128,1024]{1,0:T(8,128)S(1)} %get-tuple-element.30), channel_id=1, source_target_pairs={{0,1},{1,2},{2,3},{3,0},{4,5},{5,6},{6,7},{7,4},{8,9},{9,10},{10,1... | collective-permute-start | bytes 1572872 | tf_op jit(solution)/shard_map/ppermute | solution.py:176
  153.7 14.9 %collective-permute-start.9 = (f32[128,1024]{1,0:T(8,128)S(1)}, f32[128,1024]{1,0:T(8,128)S(1)}, u32[]{:S(2)}, u32[]{:S(2)}) collective-permute-start(f32[128,1024]{1,0:T(8,128)S(1)} %get-tuple-element.30), channel_id=1, source_target_pairs={{0,3},{1,0},{2,1},{3,2},{4,7},{5,4},{6,5},{7,6},{8,11},{9,8},{10,9... | collective-permute-start | bytes 1572872 | tf_op jit(solution)/shard_map/ppermute | solution.py:176
  169.0 5.2 %collective-permute-start.10 = (f32[256]{0:T(256)S(1)}, f32[256]{0:T(256)S(1)}, u32[]{:S(2)}, u32[]{:S(2)}) collective-permute-start(f32[256]{0:T(256)S(1)} %exponential_reduce_fusion.3), channel_id=1, source_target_pairs={{0,2},{1,3},{2,0},{3,1},{4,6},{5,7},{6,4},{7,5},{8,10},{9,11},{10,... | collective-permute-start | bytes 3080 | tf_op jit(solution)/shard_map/ppermute | solution.py:176
  170.3 4.8 %collective-permute-start.11 = (f32[256]{0:T(256)S(1)}, f32[256]{0:T(256)S(1)}, u32[]{:S(2)}, u32[]{:S(2)}) collective-permute-start(f32[256]{0:T(256)S(1)} %exponential_reduce_fusion.3), channel_id=1, source_target_pairs={{0,1},{1,2},{2,3},{3,0},{4,5},{5,6},{6,7},{7,4},{8,9},{9,10},{10,1... | collective-permute-start | bytes 3080 | tf_op jit(solution)/shard_map/ppermute | solution.py:176
  171.7 3.6 %collective-permute-start.12 = (f32[256]{0:T(256)S(1)}, f32[256]{0:T(256)S(1)}, u32[]{:S(2)}, u32[]{:S(2)}) collective-permute-start(f32[256]{0:T(256)S(1)} %exponential_reduce_fusion.3), channel_id=1, source_target_pairs={{0,3},{1,0},{2,1},{3,2},{4,7},{5,4},{6,5},{7,6},{8,11},{9,8},{10,9... | collective-permute-start | bytes 3080 | tf_op jit(solution)/shard_map/ppermute | solution.py:176
  175.6 14.7 %collective-permute-start.13 = (f32[128,1024]{1,0:T(8,128)S(1)}, f32[128,1024]{1,0:T(8,128)S(1)}, u32[]{:S(2)}, u32[]{:S(2)}) collective-permute-start(f32[128,1024]{1,0:T(8,128)S(1)} %collective-permute-done.3.left0_ref), channel_id=1, source_target_pairs={{0,1},{1,2},{2,3},{3,0},{4,5},{5,6},{6,7},{7,4},{8,9},{9,10},{10,1... | collective-permute-start | bytes 1572872 | tf_op jit(solution)/shard_map/ppermute | solution.py:176
  176.6 14.6 %collective-permute-start.14 = (f32[128,1024]{1,0:T(8,128)S(1)}, f32[128,1024]{1,0:T(8,128)S(1)}, u32[]{:S(2)}, u32[]{:S(2)}) collective-permute-start(f32[128,1024]{1,0:T(8,128)S(1)} %collective-permute-done.9.right1_ref), channel_id=1, source_target_pairs={{0,3},{1,0},{2,1},{3,2},{4,7},{5,4},{6,5},{7,6},{8,11},{9,8},{10,9... | collective-permute-start | bytes 1572872 | tf_op jit(solution)/shard_map/ppermute | solution.py:176
  190.3 0.8 copy-start.1
  192.3 5.2 %collective-permute-start.15 = (f32[256]{0:T(256)S(1)}, f32[256]{0:T(256)S(1)}, u32[]{:S(2)}, u32[]{:S(2)}) collective-permute-start(f32[256]{0:T(256)S(1)} %exponential_reduce_fusion.1), channel_id=1, source_target_pairs={{0,2},{1,3},{2,0},{3,1},{4,6},{5,7},{6,4},{7,5},{8,10},{9,11},{10,... | collective-permute-start | bytes 3080 | tf_op jit(solution)/shard_map/ppermute | solution.py:176
  193.8 4.8 %collective-permute-start.16 = (f32[256]{0:T(256)S(1)}, f32[256]{0:T(256)S(1)}, u32[]{:S(2)}, u32[]{:S(2)}) collective-permute-start(f32[256]{0:T(256)S(1)} %exponential_reduce_fusion.1), channel_id=1, source_target_pairs={{0,1},{1,2},{2,3},{3,0},{4,5},{5,6},{6,7},{7,4},{8,9},{9,10},{10,1... | collective-permute-start | bytes 3080 | tf_op jit(solution)/shard_map/ppermute | solution.py:176
  195.2 3.6 %collective-permute-start.17 = (f32[256]{0:T(256)S(1)}, f32[256]{0:T(256)S(1)}, u32[]{:S(2)}, u32[]{:S(2)}) collective-permute-start(f32[256]{0:T(256)S(1)} %exponential_reduce_fusion.1), channel_id=1, source_target_pairs={{0,3},{1,0},{2,1},{3,2},{4,7},{5,4},{6,5},{7,6},{8,11},{9,8},{10,9... | collective-permute-start | bytes 3080 | tf_op jit(solution)/shard_map/ppermute | solution.py:176
  199.8 11.6 %all-to-all-start.3 = ((f32[32,8,128]{2,1,0:T(8,128)}), f32[32,8,128]{2,1,0:T(8,128)S(1)}, u32[]{:S(2)}, u32[]{:S(2)}) async-start(f32[32,8,128]{2,1,0:T(8,128)} %broadcast_in_dim.19), calls=%async_computation.3 | async-start | bytes 262144 | tf_op jit(solution)/shard_map/all_to_all | solution.py:184
  212.1 4.8 %collective-permute-start.18 = (f32[1024]{0:T(1024)S(1)}, f32[1024]{0:T(1024)S(1)}, u32[]{:S(2)}, u32[]{:S(2)}) collective-permute-start(f32[1024]{0:T(1024)S(1)} %get-tuple-element.46), channel_id=1, source_target_pairs={{0,1},{1,2},{2,3},{3,0},{4,5},{5,6},{6,7},{7,4},{8,9},{9,10},{10,1... | collective-permute-start | bytes 12296 | tf_op jit(solution)/shard_map/ppermute | solution.py:176
  212.8 5.4 %collective-permute-start.19 = (f32[1024]{0:T(1024)S(1)}, f32[1024]{0:T(1024)S(1)}, u32[]{:S(2)}, u32[]{:S(2)}) collective-permute-start(f32[1024]{0:T(1024)S(1)} %get-tuple-element.46), channel_id=1, source_target_pairs={{0,2},{1,3},{2,0},{3,1},{4,6},{5,7},{6,4},{7,5},{8,10},{9,11},{10,... | collective-permute-start | bytes 12296 | tf_op jit(solution)/shard_map/ppermute | solution.py:176
  216.6 3.6 %collective-permute-start.20 = (f32[1024]{0:T(1024)S(1)}, f32[1024]{0:T(1024)S(1)}, u32[]{:S(2)}, u32[]{:S(2)}) collective-permute-start(f32[1024]{0:T(1024)S(1)} %get-tuple-element.46), channel_id=1, source_target_pairs={{0,3},{1,0},{2,1},{3,2},{4,7},{5,4},{6,5},{7,6},{8,11},{9,8},{10,9... | collective-permute-start | bytes 12296 | tf_op jit(solution)/shard_map/ppermute | solution.py:176
  220.2 1.0 copy-start.2
  221.3 1.0 copy-start.4
  (1 other events, 0.8 us)
Sparse Core Ops, SparseCore 0:
  10.3 85.6 all-gather.4
  98.2 76.2 all-gather.6

commit v2 on v1

v2 whole, which is shorter than its diff:
```python
import functools
import math

import jax
import jax.numpy as jnp
from jax import lax
from jax.experimental import pallas as pl
from jax.experimental.pallas import tpu as pltpu
from jax.sharding import PartitionSpec as P

ITERS = 4
EPSILON = 0.02
LOG2E = 1.0 / math.log(2.0)
SCALE = LOG2E / EPSILON
VMEM_LIMIT = 40 * 1024 * 1024


def split(v):
    hi = v.astype(jnp.bfloat16)
    return hi, (v - hi.astype(jnp.float32)).astype(jnp.bfloat16)


def split_kernel(value_ref, hi_ref, lo_ref):
    hi_ref[...], lo_ref[...] = split(value_ref[...])


def split_noise(noise):
    rows, width = noise.shape
    block = pl.BlockSpec((rows, 512), lambda i: (0, i))
    return pl.pallas_call(
        split_kernel,
        grid=(width // 512,),
        in_specs=[block],
        out_specs=[block] * 2,
        out_shape=[jax.ShapeDtypeStruct((rows, width), jnp.bfloat16)] * 2,
    )(noise)


def cross_kernel(factor, group, hi_ref, lo_ref, data_hbm, cross_ref, norm_ref, data_ref, square_ref, sems):
    blocks, cols, part = data_ref.shape
    depth = group * part
    copies = [
        pltpu.make_async_copy(
            data_hbm.at[pl.ds(i * group, group)], data_ref.at[pl.ds(i * group, group)], sems.at[i]
        )
        for i in range(blocks // group)
    ]
    for copy in copies:
        copy.start()
    for i, copy in enumerate(copies):
        copy.wait()
        values = [data_ref[i * group + j] for j in range(group)]
        joined = jnp.concatenate(values, axis=1)
        data_hi, data_lo = split(joined)
        columns = slice(i * depth, (i + 1) * depth)
        mul = functools.partial(
            lax.dot_general,
            dimension_numbers=(((1,), (1,)), ((), ())),
            preferred_element_type=jnp.float32,
        )
        noise_hi = hi_ref[:, columns]
        product = mul(noise_hi, data_hi) + (mul(noise_hi, data_lo) + mul(lo_ref[:, columns], data_hi))
        squares = sum(v * v for v in values)
        if i == 0:
            cross_ref[...] = product
            square_ref[...] = squares
        else:
            cross_ref[...] += product
            square_ref[...] += squares
    cross_ref[...] = cross_ref[...] * factor
    norm_ref[...] = lax.dot_general(
        jnp.ones((8, part), jnp.float32),
        square_ref[...],
        (((1,), (1,)), ((), ())),
        precision=lax.Precision.HIGHEST,
        preferred_element_type=jnp.float32,
    )


def cross_products(noise_hi, noise_lo, gathered):
    rows, width = noise_hi.shape
    blocks, cols, part = gathered.shape
    group = 4
    return pl.pallas_call(
        functools.partial(cross_kernel, 2.0 * SCALE / width, group),
        in_specs=[pl.BlockSpec(memory_space=pltpu.VMEM)] * 2 + [pl.BlockSpec(memory_space=pl.ANY)],
        out_specs=[pl.BlockSpec(memory_space=pltpu.VMEM)] * 2,
        out_shape=[
            jax.ShapeDtypeStruct((rows, cols), jnp.float32),
            jax.ShapeDtypeStruct((8, cols), jnp.float32),
        ],
        scratch_shapes=[
            pltpu.VMEM((blocks, cols, part), jnp.float32),
            pltpu.VMEM((cols, part), jnp.float32),
            pltpu.SemaphoreType.DMA((blocks // group,)),
        ],
        compiler_params=pltpu.CompilerParams(vmem_limit_bytes=VMEM_LIMIT),
        cost_estimate=pl.CostEstimate(
            flops=6 * rows * cols * width, bytes_accessed=4 * cols * width, transcendentals=0
        ),
    )(noise_hi, noise_lo, gathered)


def target_kernel(
    place_ref,
    noise_ref,
    data_pot_ref,
    own_ref,
    left0_hbm,
    left1_hbm,
    right0_hbm,
    right1_hbm,
    far0_hbm,
    far1_hbm,
    data_hbm,
    target_ref,
    total_ref,
    score_ref,
    data_ref,
    sums_ref,
    score_sems,
    data_sems,
):
    place = place_ref[0]
    depth = data_ref.shape[2]
    half = left0_hbm.shape[0]
    mul = functools.partial(jnp.dot, preferred_element_type=jnp.float32)
    pieces = ((left0_hbm, left1_hbm), (far0_hbm, far1_hbm), (right0_hbm, right1_hbm))
    score_copies, data_copies = [], []
    for offset in range(4):
        if offset:
            score_copies.append(
                [
                    pltpu.make_async_copy(
                        piece, score_ref.at[offset - 1, pl.ds(i * half, half)], score_sems.at[offset - 1, i]
                    )
                    for i, piece in enumerate(pieces[offset - 1])
                ]
            )
            for copy in score_copies[-1]:
                copy.start()
        for quarter in range(4):
            data_copies.append(
                pltpu.make_async_copy(
                    data_hbm.at[quarter, :, offset],
                    data_ref.at[offset * 4 + quarter],
                    data_sems.at[offset * 4 + quarter],
                )
            )
            data_copies[-1].start()
    for offset in range(4):
        if offset:
            for copy in score_copies[offset - 1]:
                copy.wait()
        folded = 0.0
        for quarter in range(4):
            step = offset * 4 + quarter
            data_copies[step].wait()
            columns = slice(quarter * depth, (quarter + 1) * depth)
            values = jnp.concatenate([data_ref[step, b] for b in range(data_ref.shape[1])], axis=1)
            data_hi, data_lo = split(values)
            scores = score_ref[offset - 1, :, columns] if offset else own_ref[:, columns]
            weight = jnp.exp2(scores + noise_ref[...] + data_pot_ref[offset, :, columns])
            folded += sum(weight[:, c : c + 128] for c in range(0, depth, 128))
            w_hi, w_lo = split(weight)
            product = mul(w_hi, data_hi) + (mul(w_hi, data_lo) + mul(w_lo, data_hi))
            if step == 0:
                target_ref[...] = product
            else:
                target_ref[...] += product
        sums_ref[lax.rem(place + 4 - offset, 4)] = folded
    total = (sums_ref[0] + sums_ref[1]) + (sums_ref[2] + sums_ref[3])
    total = jnp.sum(total, axis=1, keepdims=True)
    target_ref[...] = target_ref[...] / total
    total_ref[...] = jnp.broadcast_to(total, total_ref.shape)


def weighted_targets(place, noise_pot, data_pots, own, left, right, far, gathered):
    rows, cols = own.shape
    part = gathered.shape[-1]
    data = gathered.reshape(4, 8, 4, cols // 4, part)
    vmem, hbm = pl.BlockSpec(memory_space=pltpu.VMEM), pl.BlockSpec(memory_space=pl.ANY)
    return pl.pallas_call(
        target_kernel,
        in_specs=[pl.BlockSpec(memory_space=pltpu.SMEM)] + [vmem] * 3 + [hbm] * 7,
        out_specs=[vmem] * 2,
        out_shape=[
            jax.ShapeDtypeStruct((rows, 8 * part), jnp.float32),
            jax.ShapeDtypeStruct((rows, 128), jnp.float32),
        ],
        scratch_shapes=[
            pltpu.VMEM((3, rows, cols), jnp.float32),
            pltpu.VMEM((16, 8, cols // 4, part), jnp.float32),
            pltpu.VMEM((4, rows, 128), jnp.float32),
            pltpu.SemaphoreType.DMA((3, 2)),
            pltpu.SemaphoreType.DMA((16,)),
        ],
        compiler_params=pltpu.CompilerParams(vmem_limit_bytes=VMEM_LIMIT),
        cost_estimate=pl.CostEstimate(
            flops=24 * rows * cols * 8 * part, bytes_accessed=20 * 1024 * 1024, transcendentals=4 * rows * cols
        ),
    )(place, noise_pot, data_pots, own, *left, *right, *far, data)


def shift(v, by):
    return lax.ppermute(v, "col", [(i, (i + by) % 4) for i in range(4)])


def around(v):
    return shift(v, 1), shift(v, 2), shift(v, 3)


def spread(v):
    return lax.all_to_all(jnp.broadcast_to(v[None], (32,) + v.shape), "row", 0, 0, tiled=True)


def pair_logsum(peaks, totals):
    peak = functools.reduce(jnp.maximum, peaks)
    scaled = [t * jnp.exp2(p - peak) for p, t in zip(peaks, totals)]
    return peak + jnp.log2((scaled[0] + scaled[2]) + (scaled[1] + scaled[3]))


def local(noise, data):
    rows, width = noise.shape
    cols, part = data.shape
    rows_all, cols_all = rows * 32, cols * 4
    log_rows, log_cols = math.log2(rows_all), math.log2(cols_all)
    place = lax.axis_index("col")
    quarter = cols // 4

    gathered = lax.all_gather(data, "row", axis=0, tiled=False)

    blocks = data.reshape(4, quarter, part)
    level = lax.axis_index("row") // 8
    held = []
    for k in range(4):
        block = lax.dynamic_index_in_dim(blocks, lax.rem(level + k, 4), 0, keepdims=False)
        held.append(lax.ppermute(block, "row", [(i, (i + 8 * k) % 32) for i in range(32)]) if k else block)
    held = jnp.stack(held)
    turned = []
    for k in range(4):
        block = lax.dynamic_index_in_dim(held, lax.rem(level + 8 - place - k, 4), 0, keepdims=False)
        turned.append(shift(block, k) if k else block)
    turned = jnp.concatenate(turned, axis=0)

    noise_norm = jnp.sum(noise * noise, axis=1) / width
    parts = split_noise(noise)
    gathered, turned, parts, noise_norm = lax.optimization_barrier((gathered, turned, parts, noise_norm))
    scores, norms = cross_products(*parts, gathered)
    data_norm = norms[0] / width

    turned = lax.all_gather(turned, "row", axis=0, tiled=False)

    shifted = scores - (data_norm * SCALE)[None, :]
    peak = jnp.max(shifted, axis=1)
    total = jnp.sum(jnp.exp2(shifted - peak[:, None]), axis=1)
    pair = jnp.stack([peak, total])
    pairs = (pair,) + around(pair)
    noise_pot = -log_rows - pair_logsum([p[0] for p in pairs], [p[1] for p in pairs])

    halves = (scores[: rows // 2], scores[rows // 2 :])
    shifted = scores + noise_pot[:, None]
    peak = jnp.max(shifted, axis=0)
    total = jnp.sum(jnp.exp2(shifted - peak[None, :]), axis=0)
    pair = jnp.concatenate([peak, total]).reshape(16, 128)
    noise_pot, first = lax.optimization_barrier((noise_pot, halves[0]))
    left0, right0 = shift(first, 1), shift(first, 3)
    pairs = spread(pair)
    pairs, left0, right0 = lax.optimization_barrier((pairs, left0, right0))
    peaks, totals = pairs[:, :8].reshape(32, cols), pairs[:, 8:].reshape(32, cols)
    peak = jnp.max(peaks, axis=0)
    total = jnp.sum(totals * jnp.exp2(peaks - peak[None, :]), axis=0)
    data_pot = -log_cols - (peak + jnp.log2(total))

    for step in range(1, ITERS):
        total = jnp.sum(jnp.exp2(scores + noise_pot[:, None] + data_pot[None, :]), axis=1)
        one, two, three = around(total)
        noise_pot = noise_pot - log_rows - jnp.log2((total + two) + (one + three))
        total = jnp.sum(jnp.exp2(scores + noise_pot[:, None] + data_pot[None, :]), axis=0)
        total = total.reshape(8, 128)
        if step == 1:
            noise_pot, second = lax.optimization_barrier((noise_pot, halves[1]))
            left1, right1 = shift(second, 1), shift(second, 3)
            totals = spread(total)
            totals, left1, right1 = lax.optimization_barrier((totals, left1, right1))
        elif step == 2:
            noise_pot, left0, right1 = lax.optimization_barrier((noise_pot, left0, right1))
            far0, far1 = shift(left0, 1), shift(right1, 3)
            totals = spread(total)
            totals, far0, far1 = lax.optimization_barrier((totals, far0, far1))
        else:
            totals = spread(total)
        data_pot = data_pot - log_cols - jnp.log2(jnp.sum(totals, axis=0).reshape(cols))

    data_pots = jnp.stack((data_pot,) + around(data_pot))[:, None, :]
    targets, total = weighted_targets(
        place.reshape(1).astype(jnp.int32),
        noise_pot[:, None],
        data_pots,
        scores,
        (left0, left1),
        (right0, right1),
        (far0, far1),
        turned,
    )
    noise_pot = noise_pot - log_rows - jnp.log2(total[:, 0])
    return (targets, noise_norm + noise_pot / SCALE, data_norm + data_pot / SCALE)


def solution(mesh):
    placed = (P("row", None), P("col", "row"))
    return jax.shard_map(
        local,
        mesh=mesh,
        in_specs=placed,
        out_specs=(P("row", "col"), P("row"), P("col")),
        check_vma=False,
    )
```

time: 251 us -> 223 us (0.89)
  Pallas kernels: 37.5 us -> 27.5 us
  starting transfers between devices: 50.1 us -> 42.5 us
  waiting for transfers between devices: 90.7 us -> 83.2 us
  blocking collectives: 40.9 us -> 38 us
    ppermute x4 -> x3, waiting for transfers between devices: 18.5 us -> 0.01 us  [local(): lax.ppermute(block, 'row', [(i, (i + 8 * k) % 32) for i in range(32)])]
    ppermute x21 -> x24, waiting for transfers between devices: 11.6 us -> 26 us  [shift(): return lax.ppermute(v, 'col', [(i, (i + by) % 4) for i in range(4)])]
    pallas_call x2 -> x3, Pallas kernels: 37.5 us -> 27.5 us  [the longest x1 11.1 us: weighted_targets(): pl.pallas_call(target_kernel, in_specs=[pl.BlockSpec(memory_space=pltpu.S...]
    ppermute x4 -> x3, starting transfers between devices: 12.8 us -> 5.45 us  [local(): lax.ppermute(block, 'row', [(i, (i + 8 * k) % 32) for i in range(32)])]
    all_gather x1, waiting for transfers between devices: 54.8 us -> 48.9 us  [local(): gathered = lax.all_gather(data, 'row', axis=0, tiled=False)]
    all_to_all x3, blocking collectives: 40.9 us -> 38 us  [spread(): lax.all_to_all(jnp.broadcast_to(v[None], (32,) + v.shape), 'row', 0, 0, t...]
    all_to_all x1, waiting for transfers between devices: 5.1 us -> 7.66 us  [spread(): lax.all_to_all(jnp.broadcast_to(v[None], (32,) + v.shape), 'row', 0, 0, t...]
    unnamed x10 -> x12, local copies, waits for them, and re-layouts: 5.85 us -> 6.83 us
  transfers between devices with their start and end apart: 28 -> 30, of which waited for: 18 -> 18; matrix products, arithmetic and copies ran while one was open for 4% -> 4% of each run, Pallas kernels for 7% -> 7%
where the time goes in v2:
time: 223 us
  waiting for transfers between devices  83.2 us (37%)
  starting transfers between devices  42.5 us (19%)
  blocking collectives  38 us (17%)
  Pallas kernels  27.5 us (12%)
  between operations  14.4 us (6%)
  local copies, waits for them, and re-layouts  8.95 us (4%)
  other arithmetic  8 us (4%)
    all_gather x1, waiting for transfers between devices, local(): gathered = lax.all_gather(data, 'row', axis=0, tiled=False)  48.9 us
    all_to_all x3, blocking collectives, spread(): lax.all_to_all(jnp.broadcast_to(v[None], (32,) + v.shape), 'row', 0, 0, t...  38 us
    ppermute x24, starting transfers between devices, shift(): return lax.ppermute(v, 'col', [(i, (i + by) % 4) for i in range(4)])  33.1 us
    ppermute x24, waiting for transfers between devices, shift(): return lax.ppermute(v, 'col', [(i, (i + by) % 4) for i in range(4)])  26 us
    pallas_call x1, Pallas kernels, weighted_targets(): pl.pallas_call(target_kernel, in_specs=[pl.BlockSpec(memory_space=pltpu.S...  11.1 us
    pallas_call x1, Pallas kernels, cross_products(): pl.pallas_call(functools.partial(cross_kernel, 2.0 * SCALE / width, group...  9.58 us
    all_to_all x1, waiting for transfers between devices, spread(): lax.all_to_all(jnp.broadcast_to(v[None], (32,) + v.shape), 'row', 0, 0, t...  7.66 us
    unnamed x12, local copies, waits for them, and re-layouts  6.83 us
  transfers between devices with their start and end apart: 30, of which 18 were waited for; matrix products, arithmetic and copies ran while one was open for 4% of the time, Pallas kernels for 7%

profile of v2, /device:TPU:0, one launch (start us, length us, event | category | flops | bytes accessed | tf_op | source)
XLA Modules:
  0.0 222.5 jit_solution(8793407191139066209)
XLA Ops:
  9.2 4.2 %collective-permute-start.2 = (f32[256,128]{1,0:T(8,128)S(1)}, f32[256,128]{1,0:T(8,128)S(1)}, u32[]{:S(2)}, u32[]{:S(2)}) collective-permute-start(f32[256,128]{1,0:T(8,128)S(1)} %get-tuple-element.66), channel_id=1, source_target_pairs={{0,96},{4,100},{8,104},{12,108},{16,112},{20,116},{24,120},{28,124... | collective-permute-start | bytes 393224 | tf_op jit(solution)/shard_map/ppermute | solution.py:238
  14.6 2.5 %multiply_reduce_fusion = f32[256]{0:T(256)S(1)} fusion(f32[256,4096]{1,0:T(8,128)} %value_ref.1), kind=kLoop, calls=%fused_computation | loop fusion | flops 2096896 | bytes 4195328 | tf_op jit(solution)/shard_map/reduce_sum | solution.py:246
  17.2 6.8 %shard_map.49 = (bf16[256,4096]{1,0:T(8,128)(2,1)}, bf16[256,4096]{1,0:T(8,128)(2,1)}) custom-call(f32[256,4096]{1,0:T(8,128)} %value_ref.1), custom_call_target="tpu_custom_call" | custom-call | tf_op jit(solution)/shard_map/pallas_call | solution.py:30
  24.1 3.1 %collective-permute-start.5 = (f32[256,128]{1,0:T(8,128)S(1)}, f32[256,128]{1,0:T(8,128)S(1)}, u32[]{:S(2)}, u32[]{:S(2)}) collective-permute-start(f32[256,128]{1,0:T(8,128)S(1)} %get-tuple-element.62), channel_id=1, source_target_pairs={{0,3},{1,0},{2,1},{3,2},{4,7},{5,4},{6,5},{7,6},{8,11},{9,8},{10,9... | collective-permute-start | bytes 393224 | tf_op jit(solution)/shard_map/ppermute | solution.py:206
  28.8 3.1 %collective-permute-done.5 = f32[256,128]{1,0:T(8,128)S(1)} collective-permute-done((f32[256,128]{1,0:T(8,128)S(1)}, f32[256,128]{1,0:T(8,128)S(1)}, u32[]{:S(2)}, u32[]{:S(2)}) %collective-permute-start.5) | collective-permute-done | bytes 131104 | tf_op jit(solution)/shard_map/ppermute | solution.py:206
  32.0 2.3 %collective-permute-done.4 = f32[256,128]{1,0:T(8,128)S(1)} collective-permute-done((f32[256,128]{1,0:T(8,128)S(1)}, f32[256,128]{1,0:T(8,128)S(1)}, u32[]{:S(2)}, u32[]{:S(2)}) %collective-permute-start.4) | collective-permute-done | bytes 131104 | tf_op jit(solution)/shard_map/ppermute | solution.py:206
  36.5 48.9 %all-gather.5.cloned.1.call-done = f32[32768,128]{1,0:T(8,128)} async-done(((f32[1024,128]{1,0:T(8,128)}), f32[32768,128]{1,0:T(8,128)}) %all-gather.5.cloned.1.call-update) | async-done | bytes 16777232 | tf_op jit(solution)/shard_map/all_gather | solution.py:231
  85.4 1.6 copy-done
  87.0 1.6 copy-done.1
  88.6 9.6 %shard_map.50 = (f32[256,1024]{1,0:T(8,128)S(1)}, f32[8,1024]{1,0:T(8,128)S(1)}) custom-call(bf16[256,4096]{1,0:T(8,128)(2,1)S(1)} %copy-done, bf16[256,4096]{1,0:T(8,128)(2,1)S(1)} %copy-done.1, f32[32,1024,128]{2,1,0:T(8,128)} %bitcast.77), custom_call_target="tpu_custom_call" | custom-call | flops 6442450944 | bytes 16777216 | tf_op jit(solution)/shard_map/pallas_call | solution.py:84
  98.7 2.8 %collective-permute-start.8 = (f32[2,256]{1,0:T(2,128)S(1)}, f32[2,256]{1,0:T(2,128)S(1)}, u32[]{:S(2)}, u32[]{:S(2)}) collective-permute-start(f32[2,256]{1,0:T(2,128)S(1)} %pad_maximum_fusion.4), channel_id=1, source_target_pairs={{0,3},{1,0},{2,1},{3,2},{4,7},{5,4},{6,5},{7,6},{8,11},{9,8},{10,9... | collective-permute-start | bytes 6152 | tf_op jit(solution)/shard_map/ppermute | solution.py:206
  103.3 3.3 %collective-permute-done.7 = f32[2,256]{1,0:T(2,128)S(1)} collective-permute-done((f32[2,256]{1,0:T(2,128)S(1)}, f32[2,256]{1,0:T(2,128)S(1)}, u32[]{:S(2)}, u32[]{:S(2)}) %collective-permute-start.7) | collective-permute-done | bytes 2080 | tf_op jit(solution)/shard_map/ppermute | solution.py:206
  107.6 1.7 collective-permute-start.9
  109.8 14.1 %all_to_all.20 = f32[32,16,128]{2,1,0:T(8,128)S(1)} all-to-all(f32[32,16,128]{2,1,0:T(8,128)S(1)} %broadcast_in_dim.18), channel_id=1, replica_groups=mesh['row'=32,'col'=4] {'row'}, dimensions={0} | all-to-all | bytes 524288 | tf_op jit(solution)/shard_map/all_to_all | solution.py:214
  124.3 1.6 collective-permute-start.13
  126.4 1.5 collective-permute-start.11
  128.0 2.7 %collective-permute-done.12 = f32[256]{0:T(256)S(1)} collective-permute-done((f32[256]{0:T(256)S(1)}, f32[256]{0:T(256)S(1)}, u32[]{:S(2)}, u32[]{:S(2)}) %collective-permute-start.12) | collective-permute-done | bytes 1056 | tf_op jit(solution)/shard_map/ppermute | solution.py:206
  131.5 2.8 %collective-permute-start.15 = (f32[128,1024]{1,0:T(8,128)S(1)}, f32[128,1024]{1,0:T(8,128)S(1)}, u32[]{:S(2)}, u32[]{:S(2)}) collective-permute-start(f32[128,1024]{1,0:T(8,128)S(1)} %get-tuple-element.41), channel_id=1, source_target_pairs={{0,3},{1,0},{2,1},{3,2},{4,7},{5,4},{6,5},{7,6},{8,11},{9,8},{10,9... | collective-permute-start | bytes 1572872 | tf_op jit(solution)/shard_map/ppermute | solution.py:206
  134.6 12.7 %all_to_all.21 = f32[32,8,128]{2,1,0:T(8,128)S(1)} all-to-all(f32[32,8,128]{2,1,0:T(8,128)S(1)} %broadcast_in_dim.20), channel_id=1, replica_groups=mesh['row'=32,'col'=4] {'row'}, dimensions={0} | all-to-all | bytes 262144 | tf_op jit(solution)/shard_map/all_to_all | solution.py:214
  148.1 3.0 %collective-permute-start.18 = (f32[256]{0:T(256)S(1)}, f32[256]{0:T(256)S(1)}, u32[]{:S(2)}, u32[]{:S(2)}) collective-permute-start(f32[256]{0:T(256)S(1)} %exponential_reduce_fusion.3), channel_id=1, source_target_pairs={{0,3},{1,0},{2,1},{3,2},{4,7},{5,4},{6,5},{7,6},{8,11},{9,8},{10,9... | collective-permute-start | bytes 3080 | tf_op jit(solution)/shard_map/ppermute | solution.py:206
  151.1 1.5 collective-permute-start.16
  152.6 3.2 %collective-permute-done.17 = f32[256]{0:T(256)S(1)} collective-permute-done((f32[256]{0:T(256)S(1)}, f32[256]{0:T(256)S(1)}, u32[]{:S(2)}, u32[]{:S(2)}) %collective-permute-start.17) | collective-permute-done | bytes 1056 | tf_op jit(solution)/shard_map/ppermute | solution.py:206
  156.8 2.8 %collective-permute-start.20 = (f32[128,1024]{1,0:T(8,128)S(1)}, f32[128,1024]{1,0:T(8,128)S(1)}, u32[]{:S(2)}, u32[]{:S(2)}) collective-permute-start(f32[128,1024]{1,0:T(8,128)S(1)} %collective-permute-done.15.right1_hbm), channel_id=1, source_target_pairs={{0,3},{1,0},{2,1},{3,2},{4,7},{5,4},{6,5},{7,6},{8,11},{9,8},{10,9... | collective-permute-start | bytes 1572872 | tf_op jit(solution)/shard_map/ppermute | solution.py:206
  159.8 11.2 %all_to_all.22 = f32[32,8,128]{2,1,0:T(8,128)S(1)} all-to-all(f32[32,8,128]{2,1,0:T(8,128)S(1)} %broadcast_in_dim.22), channel_id=1, replica_groups=mesh['row'=32,'col'=4] {'row'}, dimensions={0} | all-to-all | bytes 262144 | tf_op jit(solution)/shard_map/all_to_all | solution.py:214
  173.0 2.0 collective-permute-start.23
  175.1 1.5 collective-permute-start.21
  176.7 3.2 %collective-permute-done.22 = f32[256]{0:T(256)S(1)} collective-permute-done((f32[256]{0:T(256)S(1)}, f32[256]{0:T(256)S(1)}, u32[]{:S(2)}, u32[]{:S(2)}) %collective-permute-start.22) | collective-permute-done | bytes 1056 | tf_op jit(solution)/shard_map/ppermute | solution.py:206
  181.2 3.9 %all-to-all-start.3 = ((f32[32,8,128]{2,1,0:T(8,128)}), f32[32,8,128]{2,1,0:T(8,128)S(1)}, u32[]{:S(2)}, u32[]{:S(2)}) async-start(f32[32,8,128]{2,1,0:T(8,128)} %broadcast_in_dim.25), calls=%async_computation.3 | async-start | bytes 262144 | tf_op jit(solution)/shard_map/all_to_all | solution.py:214
  185.2 7.7 %all-to-all-done.3 = f32[32,8,128]{2,1,0:T(8,128)S(1)} async-done(((f32[32,8,128]{2,1,0:T(8,128)}), f32[32,8,128]{2,1,0:T(8,128)S(1)}, u32[]{:S(2)}, u32[]{:S(2)}) %all-to-all-start.3) | async-done | bytes 131104 | tf_op jit(solution)/shard_map/all_to_all | solution.py:214
  193.5 3.2 %collective-permute-start.26 = (f32[1024]{0:T(1024)S(1)}, f32[1024]{0:T(1024)S(1)}, u32[]{:S(2)}, u32[]{:S(2)}) collective-permute-start(f32[1024]{0:T(1024)S(1)} %get-tuple-element.58), channel_id=1, source_target_pairs={{0,3},{1,0},{2,1},{3,2},{4,7},{5,4},{6,5},{7,6},{8,11},{9,8},{10,9... | collective-permute-start | bytes 12296 | tf_op jit(solution)/shard_map/ppermute | solution.py:206
  197.9 3.8 %collective-permute-done.25 = f32[1024]{0:T(1024)S(1)} collective-permute-done((f32[1024]{0:T(1024)S(1)}, f32[1024]{0:T(1024)S(1)}, u32[]{:S(2)}, u32[]{:S(2)}) %collective-permute-start.25) | collective-permute-done | bytes 4128 | tf_op jit(solution)/shard_map/ppermute | solution.py:206
  203.9 11.1 %shard_map.51 = (f32[256,1024]{1,0:T(8,128)}, f32[256,128]{1,0:T(8,128)S(1)}) custom-call(s32[1]{0:T(128)} %bitcast.place_ref, f32[256,1]{1,0:T(8,128)S(1)} %copy.6.noise_ref, f32[4,1,1024]{2,1,0:T(1,128)S(1)} %broadcast_in_dim.26.data_pot_ref, f32[256,1024]{1,0:T(8,128)S(1)} %get-tuple-element.35.own_ref, f32[128,1024]{1,0:T(8,128)S(1)} %collective-permute-done.9.left0_hbm, ...), custom_call_target="tpu_custom_call" | custom-call | flops 6442450944 | bytes 20971520 | tf_op jit(solution)/shard_map/pallas_call | solution.py:183
  (94 shorter events, 23.3 us)
Async XLA Ops:
  7.2 78.2 %all-gather.5.cloned.1.call-start = ((), (), s32[]{:S(2)}) async-start(), calls=%async_computation.4 | async-start | bytes 17301504 | tf_op jit(solution)/shard_map/all_gather | solution.py:231
  7.9 193.9 %all-gather.7.cloned.1.call-start = ((), (), s32[]{:S(2)}) async-start(), calls=%async_computation.5 | async-start | bytes 17301504 | tf_op jit(solution)/shard_map/all_gather | solution.py:252
  9.2 14.9 %collective-permute-start.2 = (f32[256,128]{1,0:T(8,128)S(1)}, f32[256,128]{1,0:T(8,128)S(1)}, u32[]{:S(2)}, u32[]{:S(2)}) collective-permute-start(f32[256,128]{1,0:T(8,128)S(1)} %get-tuple-element.66), channel_id=1, source_target_pairs={{0,96},{4,100},{8,104},{12,108},{16,112},{20,116},{24,120},{28,124... | collective-permute-start | bytes 393224 | tf_op jit(solution)/shard_map/ppermute | solution.py:238
  13.3 10.7 %collective-permute-start.1 = (f32[256,128]{1,0:T(8,128)S(1)}, f32[256,128]{1,0:T(8,128)S(1)}, u32[]{:S(2)}, u32[]{:S(2)}) collective-permute-start(f32[256,128]{1,0:T(8,128)S(1)} %get-tuple-element.67), channel_id=1, source_target_pairs={{0,64},{4,68},{8,72},{12,76},{16,80},{20,84},{24,88},{28,92},{32,9... | collective-permute-start | bytes 393224 | tf_op jit(solution)/shard_map/ppermute | solution.py:238
  13.3 10.7 %collective-permute-start = (f32[256,128]{1,0:T(8,128)S(1)}, f32[256,128]{1,0:T(8,128)S(1)}, u32[]{:S(2)}, u32[]{:S(2)}) collective-permute-start(f32[256,128]{1,0:T(8,128)S(1)} %get-tuple-element.68), channel_id=1, source_target_pairs={{0,32},{4,36},{8,40},{12,44},{16,48},{20,52},{24,56},{28,60},{32,6... | collective-permute-start | bytes 393224 | tf_op jit(solution)/shard_map/ppermute | solution.py:238
  24.1 7.8 %collective-permute-start.5 = (f32[256,128]{1,0:T(8,128)S(1)}, f32[256,128]{1,0:T(8,128)S(1)}, u32[]{:S(2)}, u32[]{:S(2)}) collective-permute-start(f32[256,128]{1,0:T(8,128)S(1)} %get-tuple-element.62), channel_id=1, source_target_pairs={{0,3},{1,0},{2,1},{3,2},{4,7},{5,4},{6,5},{7,6},{8,11},{9,8},{10,9... | collective-permute-start | bytes 393224 | tf_op jit(solution)/shard_map/ppermute | solution.py:206
  27.2 7.1 %collective-permute-start.4 = (f32[256,128]{1,0:T(8,128)S(1)}, f32[256,128]{1,0:T(8,128)S(1)}, u32[]{:S(2)}, u32[]{:S(2)}) collective-permute-start(f32[256,128]{1,0:T(8,128)S(1)} %get-tuple-element.63), channel_id=1, source_target_pairs={{0,2},{1,3},{2,0},{3,1},{4,6},{5,7},{6,4},{7,5},{8,10},{9,11},{10,... | collective-permute-start | bytes 393224 | tf_op jit(solution)/shard_map/ppermute | solution.py:206
  27.9 7.8 %collective-permute-start.3 = (f32[256,128]{1,0:T(8,128)S(1)}, f32[256,128]{1,0:T(8,128)S(1)}, u32[]{:S(2)}, u32[]{:S(2)}) collective-permute-start(f32[256,128]{1,0:T(8,128)S(1)} %get-tuple-element.64), channel_id=1, source_target_pairs={{0,1},{1,2},{2,3},{3,0},{4,5},{5,6},{6,7},{7,4},{8,9},{9,10},{10,1... | collective-permute-start | bytes 393224 | tf_op jit(solution)/shard_map/ppermute | solution.py:206
  85.4 1.6 copy-start
  87.0 1.6 copy-start.1
  98.7 4.6 %collective-permute-start.8 = (f32[2,256]{1,0:T(2,128)S(1)}, f32[2,256]{1,0:T(2,128)S(1)}, u32[]{:S(2)}, u32[]{:S(2)}) collective-permute-start(f32[2,256]{1,0:T(2,128)S(1)} %pad_maximum_fusion.4), channel_id=1, source_target_pairs={{0,3},{1,0},{2,1},{3,2},{4,7},{5,4},{6,5},{7,6},{8,11},{9,8},{10,9... | collective-permute-start | bytes 6152 | tf_op jit(solution)/shard_map/ppermute | solution.py:206
  101.5 5.1 %collective-permute-start.7 = (f32[2,256]{1,0:T(2,128)S(1)}, f32[2,256]{1,0:T(2,128)S(1)}, u32[]{:S(2)}, u32[]{:S(2)}) collective-permute-start(f32[2,256]{1,0:T(2,128)S(1)} %pad_maximum_fusion.4), channel_id=1, source_target_pairs={{0,2},{1,3},{2,0},{3,1},{4,6},{5,7},{6,4},{7,5},{8,10},{9,11},{10,... | collective-permute-start | bytes 6152 | tf_op jit(solution)/shard_map/ppermute | solution.py:206
  102.4 4.8 %collective-permute-start.6 = (f32[2,256]{1,0:T(2,128)S(1)}, f32[2,256]{1,0:T(2,128)S(1)}, u32[]{:S(2)}, u32[]{:S(2)}) collective-permute-start(f32[2,256]{1,0:T(2,128)S(1)} %pad_maximum_fusion.4), channel_id=1, source_target_pairs={{0,1},{1,2},{2,3},{3,0},{4,5},{5,6},{6,7},{7,4},{8,9},{9,10},{10,1... | collective-permute-start | bytes 6152 | tf_op jit(solution)/shard_map/ppermute | solution.py:206
  107.2 16.7 %collective-permute-start.10 = (f32[128,1024]{1,0:T(8,128)S(1)}, f32[128,1024]{1,0:T(8,128)S(1)}, u32[]{:S(2)}, u32[]{:S(2)}) collective-permute-start(f32[128,1024]{1,0:T(8,128)S(1)} %get-tuple-element.38), channel_id=1, source_target_pairs={{0,3},{1,0},{2,1},{3,2},{4,7},{5,4},{6,5},{7,6},{8,11},{9,8},{10,9... | collective-permute-start | bytes 1572872 | tf_op jit(solution)/shard_map/ppermute | solution.py:206
  107.6 16.3 %collective-permute-start.9 = (f32[128,1024]{1,0:T(8,128)S(1)}, f32[128,1024]{1,0:T(8,128)S(1)}, u32[]{:S(2)}, u32[]{:S(2)}) collective-permute-start(f32[128,1024]{1,0:T(8,128)S(1)} %get-tuple-element.38), channel_id=1, source_target_pairs={{0,1},{1,2},{2,3},{3,0},{4,5},{5,6},{6,7},{7,4},{8,9},{9,10},{10,1... | collective-permute-start | bytes 1572872 | tf_op jit(solution)/shard_map/ppermute | solution.py:206
  124.3 3.6 %collective-permute-start.13 = (f32[256]{0:T(256)S(1)}, f32[256]{0:T(256)S(1)}, u32[]{:S(2)}, u32[]{:S(2)}) collective-permute-start(f32[256]{0:T(256)S(1)} %exponential_reduce_fusion.5), channel_id=1, source_target_pairs={{0,3},{1,0},{2,1},{3,2},{4,7},{5,4},{6,5},{7,6},{8,11},{9,8},{10,9... | collective-permute-start | bytes 3080 | tf_op jit(solution)/shard_map/ppermute | solution.py:206
  125.9 4.8 %collective-permute-start.12 = (f32[256]{0:T(256)S(1)}, f32[256]{0:T(256)S(1)}, u32[]{:S(2)}, u32[]{:S(2)}) collective-permute-start(f32[256]{0:T(256)S(1)} %exponential_reduce_fusion.5), channel_id=1, source_target_pairs={{0,1},{1,2},{2,3},{3,0},{4,5},{5,6},{6,7},{7,4},{8,9},{9,10},{10,1... | collective-permute-start | bytes 3080 | tf_op jit(solution)/shard_map/ppermute | solution.py:206
  126.4 5.1 %collective-permute-start.11 = (f32[256]{0:T(256)S(1)}, f32[256]{0:T(256)S(1)}, u32[]{:S(2)}, u32[]{:S(2)}) collective-permute-start(f32[256]{0:T(256)S(1)} %exponential_reduce_fusion.5), channel_id=1, source_target_pairs={{0,2},{1,3},{2,0},{3,1},{4,6},{5,7},{6,4},{7,5},{8,10},{9,11},{10,... | collective-permute-start | bytes 3080 | tf_op jit(solution)/shard_map/ppermute | solution.py:206
  131.5 15.8 %collective-permute-start.15 = (f32[128,1024]{1,0:T(8,128)S(1)}, f32[128,1024]{1,0:T(8,128)S(1)}, u32[]{:S(2)}, u32[]{:S(2)}) collective-permute-start(f32[128,1024]{1,0:T(8,128)S(1)} %get-tuple-element.41), channel_id=1, source_target_pairs={{0,3},{1,0},{2,1},{3,2},{4,7},{5,4},{6,5},{7,6},{8,11},{9,8},{10,9... | collective-permute-start | bytes 1572872 | tf_op jit(solution)/shard_map/ppermute | solution.py:206
  134.3 13.4 %collective-permute-start.14 = (f32[128,1024]{1,0:T(8,128)S(1)}, f32[128,1024]{1,0:T(8,128)S(1)}, u32[]{:S(2)}, u32[]{:S(2)}) collective-permute-start(f32[128,1024]{1,0:T(8,128)S(1)} %get-tuple-element.41), channel_id=1, source_target_pairs={{0,1},{1,2},{2,3},{3,0},{4,5},{5,6},{6,7},{7,4},{8,9},{9,10},{10,1... | collective-permute-start | bytes 1572872 | tf_op jit(solution)/shard_map/ppermute | solution.py:206
  148.1 4.5 %collective-permute-start.18 = (f32[256]{0:T(256)S(1)}, f32[256]{0:T(256)S(1)}, u32[]{:S(2)}, u32[]{:S(2)}) collective-permute-start(f32[256]{0:T(256)S(1)} %exponential_reduce_fusion.3), channel_id=1, source_target_pairs={{0,3},{1,0},{2,1},{3,2},{4,7},{5,4},{6,5},{7,6},{8,11},{9,8},{10,9... | collective-permute-start | bytes 3080 | tf_op jit(solution)/shard_map/ppermute | solution.py:206
  151.1 4.8 %collective-permute-start.17 = (f32[256]{0:T(256)S(1)}, f32[256]{0:T(256)S(1)}, u32[]{:S(2)}, u32[]{:S(2)}) collective-permute-start(f32[256]{0:T(256)S(1)} %exponential_reduce_fusion.3), channel_id=1, source_target_pairs={{0,1},{1,2},{2,3},{3,0},{4,5},{5,6},{6,7},{7,4},{8,9},{9,10},{10,1... | collective-permute-start | bytes 3080 | tf_op jit(solution)/shard_map/ppermute | solution.py:206
  151.1 5.1 %collective-permute-start.16 = (f32[256]{0:T(256)S(1)}, f32[256]{0:T(256)S(1)}, u32[]{:S(2)}, u32[]{:S(2)}) collective-permute-start(f32[256]{0:T(256)S(1)} %exponential_reduce_fusion.3), channel_id=1, source_target_pairs={{0,2},{1,3},{2,0},{3,1},{4,6},{5,7},{6,4},{7,5},{8,10},{9,11},{10,... | collective-permute-start | bytes 3080 | tf_op jit(solution)/shard_map/ppermute | solution.py:206
  156.1 14.9 %collective-permute-start.19 = (f32[128,1024]{1,0:T(8,128)S(1)}, f32[128,1024]{1,0:T(8,128)S(1)}, u32[]{:S(2)}, u32[]{:S(2)}) collective-permute-start(f32[128,1024]{1,0:T(8,128)S(1)} %collective-permute-done.9.left0_hbm), channel_id=1, source_target_pairs={{0,1},{1,2},{2,3},{3,0},{4,5},{5,6},{6,7},{7,4},{8,9},{9,10},{10,1... | collective-permute-start | bytes 1572872 | tf_op jit(solution)/shard_map/ppermute | solution.py:206
  156.8 15.0 %collective-permute-start.20 = (f32[128,1024]{1,0:T(8,128)S(1)}, f32[128,1024]{1,0:T(8,128)S(1)}, u32[]{:S(2)}, u32[]{:S(2)}) collective-permute-start(f32[128,1024]{1,0:T(8,128)S(1)} %collective-permute-done.15.right1_hbm), channel_id=1, source_target_pairs={{0,3},{1,0},{2,1},{3,2},{4,7},{5,4},{6,5},{7,6},{8,11},{9,8},{10,9... | collective-permute-start | bytes 1572872 | tf_op jit(solution)/shard_map/ppermute | solution.py:206
  173.0 3.6 %collective-permute-start.23 = (f32[256]{0:T(256)S(1)}, f32[256]{0:T(256)S(1)}, u32[]{:S(2)}, u32[]{:S(2)}) collective-permute-start(f32[256]{0:T(256)S(1)} %exponential_reduce_fusion.1), channel_id=1, source_target_pairs={{0,3},{1,0},{2,1},{3,2},{4,7},{5,4},{6,5},{7,6},{8,11},{9,8},{10,9... | collective-permute-start | bytes 3080 | tf_op jit(solution)/shard_map/ppermute | solution.py:206
  175.0 4.8 %collective-permute-start.22 = (f32[256]{0:T(256)S(1)}, f32[256]{0:T(256)S(1)}, u32[]{:S(2)}, u32[]{:S(2)}) collective-permute-start(f32[256]{0:T(256)S(1)} %exponential_reduce_fusion.1), channel_id=1, source_target_pairs={{0,1},{1,2},{2,3},{3,0},{4,5},{5,6},{6,7},{7,4},{8,9},{9,10},{10,1... | collective-permute-start | bytes 3080 | tf_op jit(solution)/shard_map/ppermute | solution.py:206
  175.1 5.1 %collective-permute-start.21 = (f32[256]{0:T(256)S(1)}, f32[256]{0:T(256)S(1)}, u32[]{:S(2)}, u32[]{:S(2)}) collective-permute-start(f32[256]{0:T(256)S(1)} %exponential_reduce_fusion.1), channel_id=1, source_target_pairs={{0,2},{1,3},{2,0},{3,1},{4,6},{5,7},{6,4},{7,5},{8,10},{9,11},{10,... | collective-permute-start | bytes 3080 | tf_op jit(solution)/shard_map/ppermute | solution.py:206
  181.2 11.7 %all-to-all-start.3 = ((f32[32,8,128]{2,1,0:T(8,128)}), f32[32,8,128]{2,1,0:T(8,128)S(1)}, u32[]{:S(2)}, u32[]{:S(2)}) async-start(f32[32,8,128]{2,1,0:T(8,128)} %broadcast_in_dim.25), calls=%async_computation.3 | async-start | bytes 262144 | tf_op jit(solution)/shard_map/all_to_all | solution.py:214
  193.5 4.5 %collective-permute-start.26 = (f32[1024]{0:T(1024)S(1)}, f32[1024]{0:T(1024)S(1)}, u32[]{:S(2)}, u32[]{:S(2)}) collective-permute-start(f32[1024]{0:T(1024)S(1)} %get-tuple-element.58), channel_id=1, source_target_pairs={{0,3},{1,0},{2,1},{3,2},{4,7},{5,4},{6,5},{7,6},{8,11},{9,8},{10,9... | collective-permute-start | bytes 12296 | tf_op jit(solution)/shard_map/ppermute | solution.py:206
  196.6 5.1 %collective-permute-start.25 = (f32[1024]{0:T(1024)S(1)}, f32[1024]{0:T(1024)S(1)}, u32[]{:S(2)}, u32[]{:S(2)}) collective-permute-start(f32[1024]{0:T(1024)S(1)} %get-tuple-element.58), channel_id=1, source_target_pairs={{0,2},{1,3},{2,0},{3,1},{4,6},{5,7},{6,4},{7,5},{8,10},{9,11},{10,... | collective-permute-start | bytes 12296 | tf_op jit(solution)/shard_map/ppermute | solution.py:206
  196.6 5.1 %collective-permute-start.24 = (f32[1024]{0:T(1024)S(1)}, f32[1024]{0:T(1024)S(1)}, u32[]{:S(2)}, u32[]{:S(2)}) collective-permute-start(f32[1024]{0:T(1024)S(1)} %get-tuple-element.58), channel_id=1, source_target_pairs={{0,1},{1,2},{2,3},{3,0},{4,5},{5,6},{6,7},{7,4},{8,9},{9,10},{10,1... | collective-permute-start | bytes 12296 | tf_op jit(solution)/shard_map/ppermute | solution.py:206
  (4 other events, 3.7 us)
Sparse Core Ops, SparseCore 0:
  10.3 75.0 all-gather.4
  87.6 73.6 all-gather.6

commit v3 on v2

v3 whole, which is shorter than its diff:
```python
import functools
import math

import jax
import jax.numpy as jnp
from jax import lax
from jax.experimental import pallas as pl
from jax.experimental.pallas import tpu as pltpu
from jax.sharding import PartitionSpec as P

ITERS = 4
EPSILON = 0.02
LOG2E = 1.0 / math.log(2.0)
SCALE = LOG2E / EPSILON
VMEM_LIMIT = 40 * 1024 * 1024
PASSED = 512


def split(v):
    hi = v.astype(jnp.bfloat16)
    return hi, (v - hi.astype(jnp.float32)).astype(jnp.bfloat16)


def split_kernel(place_ref, own_hbm, other_hbm, hi_ref, lo_ref, held_ref, sems):
    rows, part = held_ref.shape[2:]
    copies = []
    for n in range(16):
        block = lax.rem(place_ref[0] + 4 - n // 4, 4) * 4 + lax.rem(place_ref[1] + 4 - n % 4, 4)
        columns = pl.ds(pl.multiple_of((block * 2 + place_ref[2]) * part, part), part)
        for i, noise in enumerate((own_hbm, other_hbm)):
            copies.append(pltpu.make_async_copy(noise.at[:, columns], held_ref.at[n, i], sems.at[n, i]))
            copies[-1].start()
    for n in range(16):
        for i in range(2):
            copies[2 * n + i].wait()
            hi, lo = split(held_ref[n, i])
            hi_ref[i * rows : (i + 1) * rows, n * part : (n + 1) * part] = hi
            lo_ref[i * rows : (i + 1) * rows, n * part : (n + 1) * part] = lo


def split_noise(place, own, other):
    rows, width = own.shape
    part = width // 32
    vmem, hbm = pl.BlockSpec(memory_space=pltpu.VMEM), pl.BlockSpec(memory_space=pltpu.HBM)
    return pl.pallas_call(
        split_kernel,
        in_specs=[pl.BlockSpec(memory_space=pltpu.SMEM), hbm, hbm],
        out_specs=[vmem] * 2,
        out_shape=[jax.ShapeDtypeStruct((2 * rows, 16 * part), jnp.bfloat16)] * 2,
        scratch_shapes=[pltpu.VMEM((16, 2, rows, part), jnp.float32), pltpu.SemaphoreType.DMA((16, 2))],
        compiler_params=pltpu.CompilerParams(vmem_limit_bytes=8 * 1024 * 1024),
        cost_estimate=pl.CostEstimate(flops=0, bytes_accessed=16 * 1024 * 1024, transcendentals=0),
    )(place, own, other)


def block_product(hi_ref, lo_ref, blocks, values):
    part = values[0].shape[1]
    pick = lambda ref: jnp.concatenate([ref[:, n * part : (n + 1) * part] for n in blocks], axis=1)
    noise_hi, noise_lo = pick(hi_ref), pick(lo_ref)
    data_hi, data_lo = split(jnp.concatenate(values, axis=1))
    mul = functools.partial(
        lax.dot_general, dimension_numbers=(((1,), (1,)), ((), ())), preferred_element_type=jnp.float32
    )
    return mul(noise_hi, data_hi) + (mul(noise_hi, data_lo) + mul(noise_lo, data_hi))


def ring_squares(values):
    return (values[0] * values[0] + values[2] * values[2]) + (values[1] * values[1] + values[3] * values[3])


def block_number(first, across, along):
    return across * 4 + along if first == "x" else along * 4 + across


def near_kernel(hi_ref, lo_ref, *refs):
    cross_ref, even_ref, odd_ref = refs[6:]
    for half, (first, lines) in enumerate((("x", refs[:3]), ("z", refs[3:6]))):
        cols = lines[0].shape[1]
        place = slice(half * cols, (half + 1) * cols)
        squares = []
        for line, across in zip(lines, (0, 1, 3)):
            values = [line[n] for n in range(4)]
            numbers = [block_number(first, across, n) for n in range(4)]
            product = block_product(hi_ref, lo_ref, numbers, values)
            if across == 0:
                cross_ref[:, place] = product
            else:
                cross_ref[:, place] += product
            squares.append(ring_squares(values))
        even_ref[place, :] = squares[0]
        odd_ref[place, :] = squares[1] + squares[2]


def far_kernel(factor, hi_ref, lo_ref, cross_ref, even_ref, odd_ref, x0, x1, z0, z1, own_ref, other_ref, norm_ref):
    rows = own_ref.shape[0]
    for half, (first, refs) in enumerate((("x", (x0, x1)), ("z", (z0, z1)))):
        cols = refs[0].shape[1]
        place = slice(half * cols, (half + 1) * cols)
        values = [refs[i // 2][i % 2] for i in range(4)]
        numbers = [block_number(first, 2, i) for i in range(4)]
        product = (cross_ref[:, place] + block_product(hi_ref, lo_ref, numbers, values)) * factor
        own_ref[:, place] = product[:rows]
        other_ref[:rows, place] = product[rows:]
        squares = (even_ref[place, :] + ring_squares(values)) + odd_ref[place, :]
        norms = lax.dot_general(
            jnp.ones((8, squares.shape[1]), jnp.float32),
            squares,
            (((1,), (1,)), ((), ())),
            precision=lax.Precision.HIGHEST,
            preferred_element_type=jnp.float32,
        )
        norm_ref[:, place] = norms
        other_ref[rows:, place] = norms


def products_call(kernel, share, operands, out_shapes):
    vmem = pl.BlockSpec(memory_space=pltpu.VMEM)
    rows, width = operands[0].shape
    return pl.pallas_call(
        kernel,
        in_specs=[vmem] * len(operands),
        out_specs=[vmem] * len(out_shapes),
        out_shape=[jax.ShapeDtypeStruct(dims, jnp.float32) for dims in out_shapes],
        compiler_params=pltpu.CompilerParams(vmem_limit_bytes=14 * 1024 * 1024),
        cost_estimate=pl.CostEstimate(
            flops=share * 6 * rows * 256 * width, bytes_accessed=share * 1024 * 1024, transcendentals=0
        ),
    )(*operands)


def near_products(parts, along_x, along_z):
    rows = parts[0].shape[0]
    _, cols, part = along_x[0].shape
    near = [v for q in (along_x, along_z) for v in (q[0], q[1], q[4])]
    return products_call(near_kernel, 3, (*parts, *near), [(rows, 2 * cols), (2 * cols, part), (2 * cols, part)])


def far_products(factor, parts, sums, along_x, along_z):
    rows = parts[0].shape[0]
    _, cols, part = along_x[0].shape
    far = [v for q in (along_x, along_z) for v in q[2:4]]
    shapes = [(rows // 2, 2 * cols), (rows // 2 + 8, 2 * cols), (8, 2 * cols)]
    return products_call(functools.partial(far_kernel, factor), 1, (*parts, *sums, *far), shapes)


def whole_split_kernel(value_ref, hi_ref, lo_ref):
    hi_ref[...], lo_ref[...] = split(value_ref[...])


def whole_split(noise):
    rows, width = noise.shape
    block = pl.BlockSpec((rows, 1024), lambda i: (0, i))
    return pl.pallas_call(
        whole_split_kernel,
        grid=(width // 1024,),
        in_specs=[block],
        out_specs=[block] * 2,
        out_shape=[jax.ShapeDtypeStruct((rows, width), jnp.bfloat16)] * 2,
        cost_estimate=pl.CostEstimate(flops=0, bytes_accessed=12 * 1024 * 1024, transcendentals=0),
    )(noise)


def finish_kernel(
    factor,
    group,
    own_ref,
    taken_ref,
    norm_ref,
    hi_hbm,
    lo_hbm,
    data_hbm,
    cross_ref,
    norms_ref,
    hi_ref,
    lo_ref,
    data_ref,
    square_ref,
    sems,
):
    rows, done = own_ref.shape
    blocks, cols, part = data_ref.shape
    depth = group * part
    copies = []
    for i in range(blocks // group):
        columns = pl.ds(i * depth, depth)
        held = pl.ds(i * group, group)
        copies.append(
            [
                pltpu.make_async_copy(data_hbm.at[held], data_ref.at[held], sems.at[i, 0]),
                pltpu.make_async_copy(hi_hbm.at[:, columns], hi_ref.at[:, columns], sems.at[i, 1]),
                pltpu.make_async_copy(lo_hbm.at[:, columns], lo_ref.at[:, columns], sems.at[i, 2]),
            ]
        )
        for copy in copies[-1]:
            copy.start()
    cross_ref[:, :done] = own_ref[...] + taken_ref[:rows, :]
    norms_ref[:, :done] = norm_ref[...] + taken_ref[rows:, :]
    for i in range(blocks // group):
        for copy in copies[i]:
            copy.wait()
        values = [data_ref[i * group + j] for j in range(group)]
        product = block_product(hi_ref, lo_ref, range(i * group, (i + 1) * group), values)
        squares = sum(v * v for v in values)
        if i == 0:
            cross_ref[:, done:] = product
            square_ref[...] = squares
        else:
            cross_ref[:, done:] += product
            square_ref[...] += squares
    cross_ref[:, done:] = cross_ref[:, done:] * factor
    norms_ref[:, done:] = lax.dot_general(
        jnp.ones((8, part), jnp.float32),
        square_ref[...],
        (((1,), (1,)), ((), ())),
        precision=lax.Precision.HIGHEST,
        preferred_element_type=jnp.float32,
    )


def finish_products(factor, parts, own, taken, norms, gathered):
    rows, width = parts[0].shape
    blocks, cols, part = gathered.shape
    total = own.shape[1] + cols
    group = 4
    vmem = pl.BlockSpec(memory_space=pltpu.VMEM)
    return pl.pallas_call(
        functools.partial(finish_kernel, factor, group),
        in_specs=[vmem] * 3 + [pl.BlockSpec(memory_space=pltpu.HBM)] * 3,
        out_specs=[vmem] * 2,
        out_shape=[
            jax.ShapeDtypeStruct((rows, total), jnp.float32),
            jax.ShapeDtypeStruct((8, total), jnp.float32),
        ],
        scratch_shapes=[
            pltpu.VMEM((rows, width), jnp.bfloat16),
            pltpu.VMEM((rows, width), jnp.bfloat16),
            pltpu.VMEM((blocks, cols, part), jnp.float32),
            pltpu.VMEM((cols, part), jnp.float32),
            pltpu.SemaphoreType.DMA((blocks // group, 3)),
        ],
        compiler_params=pltpu.CompilerParams(vmem_limit_bytes=VMEM_LIMIT),
        cost_estimate=pl.CostEstimate(
            flops=6 * rows * cols * width, bytes_accessed=4 * cols * width, transcendentals=0
        ),
    )(own, taken, norms, *parts, gathered)


def target_kernel(
    place_ref,
    noise_ref,
    data_pot_ref,
    own_ref,
    one_ref,
    two_ref,
    three_ref,
    data_hbm,
    target_ref,
    total_ref,
    data_ref,
    sums_ref,
    data_sems,
):
    place = place_ref[0]
    depth = data_ref.shape[2]
    mul = functools.partial(jnp.dot, preferred_element_type=jnp.float32)
    near = 1 + 2 * place_ref[1]
    pieces = ((own_ref, 0), (one_ref, near), (two_ref, 4 - near), (three_ref, 2))
    data_copies = []
    for step, (_, offset) in enumerate(pieces):
        for quarter in range(4):
            data_copies.append(
                pltpu.make_async_copy(
                    data_hbm.at[quarter, :, offset],
                    data_ref.at[step * 4 + quarter],
                    data_sems.at[step * 4 + quarter],
                )
            )
            data_copies[-1].start()
    for step, (score_ref, offset) in enumerate(pieces):
        folded = 0.0
        for quarter in range(4):
            copied = step * 4 + quarter
            data_copies[copied].wait()
            columns = slice(quarter * depth, (quarter + 1) * depth)
            values = jnp.concatenate([data_ref[copied, b] for b in range(data_ref.shape[1])], axis=1)
            data_hi, data_lo = split(values)
            weight = jnp.exp2(score_ref[:, columns] + noise_ref[...] + data_pot_ref[offset, :, columns])
            folded += sum(weight[:, c : c + 128] for c in range(0, depth, 128))
            w_hi, w_lo = split(weight)
            product = mul(w_hi, data_hi) + (mul(w_hi, data_lo) + mul(w_lo, data_hi))
            if copied == 0:
                target_ref[...] = product
            else:
                target_ref[...] += product
        sums_ref[lax.rem(place + 4 - offset, 4)] = folded
    total = (sums_ref[0] + sums_ref[1]) + (sums_ref[2] + sums_ref[3])
    total = jnp.sum(total, axis=1, keepdims=True)
    target_ref[...] = target_ref[...] / total
    total_ref[...] = jnp.broadcast_to(total, total_ref.shape)


def weighted_targets(place, noise_pot, data_pots, own, others, gathered):
    rows, cols = own.shape
    part = gathered.shape[-1]
    data = gathered.reshape(4, 8, 4, cols // 4, part)
    vmem, hbm = pl.BlockSpec(memory_space=pltpu.VMEM), pl.BlockSpec(memory_space=pl.ANY)
    return pl.pallas_call(
        target_kernel,
        in_specs=[pl.BlockSpec(memory_space=pltpu.SMEM)] + [vmem] * 6 + [hbm],
        out_specs=[vmem] * 2,
        out_shape=[
            jax.ShapeDtypeStruct((rows, 8 * part), jnp.float32),
            jax.ShapeDtypeStruct((rows, 128), jnp.float32),
        ],
        scratch_shapes=[
            pltpu.VMEM((16, 8, cols // 4, part), jnp.float32),
            pltpu.VMEM((4, rows, 128), jnp.float32),
            pltpu.SemaphoreType.DMA((16,)),
        ],
        compiler_params=pltpu.CompilerParams(vmem_limit_bytes=VMEM_LIMIT),
        cost_estimate=pl.CostEstimate(
            flops=24 * rows * cols * 8 * part, bytes_accessed=20 * 1024 * 1024, transcendentals=4 * rows * cols
        ),
    )(place, noise_pot, data_pots, own, *others, data)


def shift(v, by):
    return lax.ppermute(v, "col", [(i, (i + by) % 4) for i in range(4)])


def shift_z(v, by):
    return lax.ppermute(v, "row", [(i, (i + 8 * by) % 32) for i in range(32)])


def shift_x(v, by):
    return lax.ppermute(v, "row", [(i, i // 8 * 8 + (i + 2 * by) % 8) for i in range(32)])


def swap_cores(v):
    return lax.ppermute(v, "row", [(i, i ^ 1) for i in range(32)])


def gather_line(v, move):
    half = v.shape[0] // 2
    left, right = move(v, 1), move(v, 3)
    return v, left, move(left[:half], 1), move(right[half:], 3), right


def gather_plane(line, move):
    own, left, far0, far1, right = line
    return gather_line(jnp.stack([own, left, jnp.concatenate([far0, far1]), right]), move)


def shift_cores(v, by):
    pairs = []
    for i in range(32):
        step = 4 - by if i % 2 else by
        pairs += [(4 * i + y, 4 * i + (y + step) % 4) for y in range(4)]
    return lax.ppermute(v, ("row", "col"), pairs)


def around(v):
    return shift(v, 1), shift(v, 2), shift(v, 3)


def spread(v):
    return lax.all_to_all(jnp.broadcast_to(v[None], (32,) + v.shape), "row", 0, 0, tiled=True)


def pair_logsum(peaks, totals):
    peak = functools.reduce(jnp.maximum, peaks)
    scaled = [t * jnp.exp2(p - peak) for p, t in zip(peaks, totals)]
    return peak + jnp.log2((scaled[0] + scaled[2]) + (scaled[1] + scaled[3]))


def local(noise, data):
    rows, width = noise.shape
    cols, part = data.shape
    rows_all, cols_all = rows * 32, cols * 4
    log_rows, log_cols = math.log2(rows_all), math.log2(cols_all)
    place = lax.axis_index("col")
    quarter = cols // 4
    index = lax.axis_index("row")
    level, core = index // 8, index % 2

    gathered = lax.all_gather(data[PASSED:], "row", axis=0, tiled=False)
    line_x = gather_line(data[: PASSED // 2], shift_x)
    line_z = gather_line(data[PASSED // 2 : PASSED], shift_z)
    line_x, line_z, late_noise = lax.optimization_barrier((line_x, line_z, noise))
    along_x = gather_plane(line_x, shift_z)
    along_z = gather_plane(line_z, shift_x)

    spot = jnp.stack([level, index % 8 // 2, core]).astype(jnp.int32)
    parts = split_noise(spot, late_noise, swap_cores(late_noise))
    noise_norm = jnp.sum(late_noise * late_noise, axis=1) / width
    whole = whole_split(late_noise)

    blocks = data.reshape(4, quarter, part)
    held = []
    for k in range(4):
        block = lax.dynamic_index_in_dim(blocks, lax.rem(level + k, 4), 0, keepdims=False)
        held.append(shift_z(block, k) if k else block)
    held = jnp.stack(held)
    turned = []
    for k in range(4):
        block = lax.dynamic_index_in_dim(held, lax.rem(level + 8 - place - k, 4), 0, keepdims=False)
        turned.append(shift(block, k) if k else block)
    turned = jnp.concatenate(turned, axis=0)

    sums = near_products(parts, along_x, along_z)
    own, given, norms = far_products(2.0 * SCALE / width, parts, sums, along_x, along_z)
    taken = swap_cores(given)
    whole, gathered, turned, taken, noise_norm = lax.optimization_barrier(
        (whole, gathered, turned, taken, noise_norm)
    )
    scores, norms = finish_products(2.0 * SCALE / width, whole, own, taken, norms, gathered)
    data_norm = norms[0] / width

    turned = lax.all_gather(turned, "row", axis=0, tiled=False)

    shifted = scores - (data_norm * SCALE)[None, :]
    peak = jnp.max(shifted, axis=1)
    total = jnp.sum(jnp.exp2(shifted - peak[:, None]), axis=1)
    pair = jnp.stack([peak, total])
    pairs = (pair,) + around(pair)
    noise_pot = -log_rows - pair_logsum([p[0] for p in pairs], [p[1] for p in pairs])

    shifted = scores + noise_pot[:, None]
    peak = jnp.max(shifted, axis=0)
    total = jnp.sum(jnp.exp2(shifted - peak[None, :]), axis=0)
    pair = jnp.concatenate([peak, total]).reshape(16, 128)
    pair, mine = lax.optimization_barrier((pair, scores))
    one = shift_cores(mine, 1)
    pairs = spread(pair)
    pairs, one = lax.optimization_barrier((pairs, one))
    peaks, totals = pairs[:, :8].reshape(32, cols), pairs[:, 8:].reshape(32, cols)
    peak = jnp.max(peaks, axis=0)
    total = jnp.sum(totals * jnp.exp2(peaks - peak[None, :]), axis=0)
    data_pot = -log_cols - (peak + jnp.log2(total))

    for step in range(1, ITERS):
        total = jnp.sum(jnp.exp2(scores + noise_pot[:, None] + data_pot[None, :]), axis=1)
        before, across, after = around(total)
        noise_pot = noise_pot - log_rows - jnp.log2((total + across) + (before + after))
        total = jnp.sum(jnp.exp2(scores + noise_pot[:, None] + data_pot[None, :]), axis=0)
        total = total.reshape(8, 128)
        if step == 1:
            total, mine = lax.optimization_barrier((total, scores))
            two = shift_cores(mine, 3)
            totals = spread(total)
            totals, two = lax.optimization_barrier((totals, two))
        elif step == 2:
            total, one = lax.optimization_barrier((total, one))
            three = shift_cores(one, 1)
            totals = spread(total)
            totals, three = lax.optimization_barrier((totals, three))
        else:
            totals = spread(total)
        data_pot = data_pot - log_cols - jnp.log2(jnp.sum(totals, axis=0).reshape(cols))

    data_pots = jnp.stack((data_pot,) + around(data_pot))[:, None, :]
    targets, total = weighted_targets(
        jnp.stack([place, core]).astype(jnp.int32),
        noise_pot[:, None],
        data_pots,
        scores,
        (one, two, three),
        turned,
    )
    noise_pot = noise_pot - log_rows - jnp.log2(total[:, 0])
    return (targets, noise_norm + noise_pot / SCALE, data_norm + data_pot / SCALE)


def solution(mesh):
    placed = (P("row", None), P("col", "row"))
    return jax.shard_map(
        local,
        mesh=mesh,
        in_specs=placed,
        out_specs=(P("row", "col"), P("row"), P("col")),
        check_vma=False,
    )
```

time: 223 us -> 216 us (0.969)
  waiting for transfers between devices: 83.2 us -> 49.1 us
  starting transfers between devices: 42.5 us -> 62.6 us
  local copies, waits for them, and re-layouts: 8.95 us -> 15.3 us
  Pallas kernels: 27.5 us -> 30.2 us
    all_gather x1, waiting for transfers between devices: 48.9 us -> 0.01 us  [local(): gathered = lax.all_gather(data[PASSED:], 'row', axis=0, tiled=False)]
    ppermute x3 -> x24, waiting for transfers between devices: 0.01 us -> 28.8 us  [the longest x11 13.4 us: shift_z(): return lax.ppermute(v, 'row', [(i, (i + 8 * by) % 32) for i in range(32)])]
    ppermute x3 -> x24, starting transfers between devices: 5.45 us -> 32.5 us  [the longest x11 14.6 us: shift_z(): return lax.ppermute(v, 'row', [(i, (i + 8 * by) % 32) for i in range(32)])]
    ppermute x24 -> x18, waiting for transfers between devices: 26 us -> 12.7 us  [shift(): return lax.ppermute(v, 'col', [(i, (i + by) % 4) for i in range(4)])]
    ppermute x24 -> x18, starting transfers between devices: 33.1 us -> 26.2 us  [shift(): return lax.ppermute(v, 'col', [(i, (i + by) % 4) for i in range(4)])]
    unnamed x12 -> x22, local copies, waits for them, and re-layouts: 6.83 us -> 9.83 us
    slice x1 -> x10, local copies, waits for them, and re-layouts: 0.07 us -> 2.77 us  [the longest x1 1.69 us: local(): gathered = lax.all_gather(data[PASSED:], 'row', axis=0, tiled=False)]
    pallas_call x2 -> x5, Pallas kernels: 16.4 us -> 18.5 us  [the longest x1 5.84 us: finish_products(): pl.pallas_call(functools.partial(finish_kernel, factor, group), in_specs=...]
  transfers between devices with their start and end apart: 30 -> 45, of which waited for: 18 -> 22; matrix products, arithmetic and copies ran while one was open for 4% -> 5% of each run, Pallas kernels for 7% -> 9%
where the time goes in v3:
time: 216 us
  starting transfers between devices  62.6 us (29%)
  waiting for transfers between devices  49.1 us (23%)
  blocking collectives  36.6 us (17%)
  Pallas kernels  30.2 us (14%)
  local copies, waits for them, and re-layouts  15.3 us (7%)
  between operations  14.4 us (7%)
  other arithmetic  7.62 us (4%)
    all_to_all x3, blocking collectives, spread(): lax.all_to_all(jnp.broadcast_to(v[None], (32,) + v.shape), 'row', 0, 0, t...  36.6 us
    ppermute x18, starting transfers between devices, shift(): return lax.ppermute(v, 'col', [(i, (i + by) % 4) for i in range(4)])  26.2 us
    ppermute x11, starting transfers between devices, shift_z(): return lax.ppermute(v, 'row', [(i, (i + 8 * by) % 32) for i in range(32)])  14.6 us
    ppermute x8, starting transfers between devices, shift_x(): lax.ppermute(v, 'row', [(i, i // 8 * 8 + (i + 2 * by) % 8) for i in range...  13.9 us
    ppermute x11, waiting for transfers between devices, shift_z(): return lax.ppermute(v, 'row', [(i, (i + 8 * by) % 32) for i in range(32)])  13.4 us
    ppermute x18, waiting for transfers between devices, shift(): return lax.ppermute(v, 'col', [(i, (i + by) % 4) for i in range(4)])  12.7 us
    pallas_call x1, Pallas kernels, weighted_targets(): pl.pallas_call(target_kernel, in_specs=[pl.BlockSpec(memory_space=pltpu.S...  11.6 us
    unnamed x22, local copies, waits for them, and re-layouts  9.83 us
  transfers between devices with their start and end apart: 45, of which 22 were waited for; matrix products, arithmetic and copies ran while one was open for 5% of the time, Pallas kernels for 9%

profile of v3, /device:TPU:0, one launch (start us, length us, event | category | flops | bytes accessed | tf_op | source)
XLA Modules:
  0.0 215.7 jit_solution(9712358457203158766)
XLA Ops:
  15.3 2.1 collective-permute-start.6
  17.8 3.0 %collective-permute-start.3 = (f32[128,128]{1,0:T(8,128)S(1)}, f32[128,128]{1,0:T(8,128)S(1)}, u32[]{:S(2)}, u32[]{:S(2)}) collective-permute-start(f32[128,128]{1,0:T(8,128)S(1)} %slice.85), channel_id=1, source_target_pairs={{0,24},{4,28},{8,0},{12,4},{16,8},{20,12},{24,16},{28,20},{32,56},... | collective-permute-start | bytes 196616 | tf_op jit(solution)/shard_map/ppermute | solution.py:336
  21.9 2.3 %collective-permute-start.7 = (f32[128,128]{1,0:T(8,128)S(1)}, f32[128,128]{1,0:T(8,128)S(1)}, u32[]{:S(2)}, u32[]{:S(2)}) collective-permute-start(f32[128,128]{1,0:T(8,128)S(1)} %slice.87), channel_id=1, source_target_pairs={{0,96},{4,100},{8,104},{12,108},{16,112},{20,116},{24,120},{28,124... | collective-permute-start | bytes 196616 | tf_op jit(solution)/shard_map/ppermute | solution.py:332
  24.2 2.2 collective-permute-done.5
  32.3 2.1 collective-permute-start.19
  34.7 2.7 %collective-permute-done.17 = f32[256,128]{1,0:T(8,128)S(1)} collective-permute-done((f32[256,128]{1,0:T(8,128)S(1)}, f32[256,128]{1,0:T(8,128)S(1)}, u32[]{:S(2)}, u32[]{:S(2)}) %collective-permute-start.17) | collective-permute-done | bytes 131104 | tf_op jit(solution)/shard_map/ppermute | solution.py:332
  38.2 2.4 %collective-permute-done.18 = f32[256,128]{1,0:T(8,128)S(1)} collective-permute-done((f32[256,128]{1,0:T(8,128)S(1)}, f32[256,128]{1,0:T(8,128)S(1)}, u32[]{:S(2)}, u32[]{:S(2)}) %collective-permute-start.18) | collective-permute-done | bytes 131104 | tf_op jit(solution)/shard_map/ppermute | solution.py:332
  41.4 2.5 %collective-permute-start.12 = (f32[4,256,128]{2,1,0:T(8,128)S(1)}, f32[4,256,128]{2,1,0:T(8,128)S(1)}, u32[]{:S(2)}, u32[]{:S(2)}) collective-permute-start(f32[4,256,128]{2,1,0:T(8,128)S(1)} %pad_maximum_fusion.1.refs_3_), channel_id=1, source_target_pairs={{0,24},{4,28},{8,0},{12,4},{16,8},{20,12},{24,16},{28,20},{32,56},... | collective-permute-start | bytes 1572872 | tf_op jit(solution)/shard_map/ppermute | solution.py:336
  45.6 4.8 %shard_map.52 = (bf16[256,4096]{1,0:T(8,128)(2,1)}, bf16[256,4096]{1,0:T(8,128)(2,1)}) custom-call(f32[256,4096]{1,0:T(8,128)} %value_ref), custom_call_target="tpu_custom_call" | custom-call | bytes 12582912 | tf_op jit(solution)/shard_map/pallas_call | solution.py:153
  50.4 5.2 %collective-permute-done.9.refs_1_ = f32[4,256,128]{2,1,0:T(8,128)S(1)} collective-permute-done((f32[4,256,128]{2,1,0:T(8,128)S(1)}, f32[4,256,128]{2,1,0:T(8,128)S(1)}, u32[]{:S(2)}, u32[]{:S(2)}) %collective-permute-start.9) | collective-permute-done | bytes 524320 | tf_op jit(solution)/shard_map/ppermute | solution.py:332
  57.1 4.5 %collective-permute-done.11.refs_4_ = f32[4,256,128]{2,1,0:T(8,128)S(1)} collective-permute-done((f32[4,256,128]{2,1,0:T(8,128)S(1)}, f32[4,256,128]{2,1,0:T(8,128)S(1)}, u32[]{:S(2)}, u32[]{:S(2)}) %collective-permute-start.11) | collective-permute-done | bytes 524320 | tf_op jit(solution)/shard_map/ppermute | solution.py:336
  61.6 2.7 %collective-permute-done.12.refs_5_ = f32[4,256,128]{2,1,0:T(8,128)S(1)} collective-permute-done((f32[4,256,128]{2,1,0:T(8,128)S(1)}, f32[4,256,128]{2,1,0:T(8,128)S(1)}, u32[]{:S(2)}, u32[]{:S(2)}) %collective-permute-start.12) | collective-permute-done | bytes 524320 | tf_op jit(solution)/shard_map/ppermute | solution.py:336
  64.3 3.9 %collective-permute-start.16 = (f32[2,256,128]{2,1,0:T(8,128)S(1)}, f32[2,256,128]{2,1,0:T(8,128)S(1)}, u32[]{:S(2)}, u32[]{:S(2)}) collective-permute-start(f32[2,256,128]{2,1,0:T(8,128)S(1)} %slice.91), channel_id=1, source_target_pairs={{0,24},{4,28},{8,0},{12,4},{16,8},{20,12},{24,16},{28,20},{32,56},... | collective-permute-start | bytes 786440 | tf_op jit(solution)/shard_map/ppermute | solution.py:336
  68.3 2.4 %copy-done = f32[256,4096]{1,0:T(8,128)S(1)} copy-done((f32[256,4096]{1,0:T(8,128)S(1)}, f32[256,4096]{1,0:T(8,128)}, u32[]{:S(2)}) %copy-start) | copy-done | bytes 4194328
  70.6 2.9 %shard_map.49 = (bf16[512,2048]{1,0:T(8,128)(2,1)S(1)}, bf16[512,2048]{1,0:T(8,128)(2,1)S(1)}) custom-call(s32[3]{0:T(128)S(1)} %pad_add_fusion.1.place_ref, f32[256,4096]{1,0:T(8,128)S(1)} %copy-done, f32[256,4096]{1,0:T(8,128)} %collective-permute-done.8.other_hbm), custom_call_target="tpu_custom_call" | custom-call | bytes 16777216 | tf_op jit(solution)/shard_map/pallas_call | solution.py:45
  73.6 2.8 %shard_map.50 = (f32[512,512]{1,0:T(8,128)S(1)}, f32[512,128]{1,0:T(8,128)S(1)}, f32[512,128]{1,0:T(8,128)S(1)}) custom-call(bf16[512,2048]{1,0:T(8,128)(2,1)S(1)} %get-tuple-element.47.hi_ref, bf16[512,2048]{1,0:T(8,128)(2,1)S(1)} %get-tuple-element.48.lo_ref, f32[4,256,128]{2,1,0:T(8,128)S(1)} %pad_maximum_fusion.refs_0_, ...), custom_call_target="tpu_custom_call" | custom-call | flops 4831838208 | bytes 3145728 | tf_op jit(solution)/shard_map/pallas_call | solution.py:119
  76.4 2.8 %collective-permute-start.21 = (f32[256,128]{1,0:T(8,128)S(1)}, f32[256,128]{1,0:T(8,128)S(1)}, u32[]{:S(2)}, u32[]{:S(2)}) collective-permute-start(f32[256,128]{1,0:T(8,128)S(1)} %get-tuple-element.95), channel_id=1, source_target_pairs={{0,2},{1,3},{2,0},{3,1},{4,6},{5,7},{6,4},{7,5},{8,10},{9,11},{10,... | collective-permute-start | bytes 393224 | tf_op jit(solution)/shard_map/ppermute | solution.py:328
  90.1 5.8 %shard_map.53 = (f32[256,1024]{1,0:T(8,128)S(1)}, f32[8,1024]{1,0:T(8,128)S(1)}) custom-call(f32[256,512]{1,0:T(8,128)S(1)} %copy-done.7, f32[264,512]{1,0:T(8,128)S(1)} %copy-done.5, f32[8,512]{1,0:T(8,128)S(1)} %get-tuple-element.67.norm_ref, bf16[256,4096]{1,0:T(8,128)(2,1)S(1)} %copy-done.2, bf16[256,4096]{1,0:T(8,128)(2,1)S(1)} %copy-done.3, ...), custom_call_target="tpu_custom_call" | custom-call | flops 3221225472 | bytes 8388608 | tf_op jit(solution)/shard_map/pallas_call | solution.py:226
  97.7 2.7 %collective-permute-start.25 = (f32[2,256]{1,0:T(2,128)S(1)}, f32[2,256]{1,0:T(2,128)S(1)}, u32[]{:S(2)}, u32[]{:S(2)}) collective-permute-start(f32[2,256]{1,0:T(2,128)S(1)} %pad_maximum_fusion.6), channel_id=1, source_target_pairs={{0,2},{1,3},{2,0},{3,1},{4,6},{5,7},{6,4},{7,5},{8,10},{9,11},{10,... | collective-permute-start | bytes 6152 | tf_op jit(solution)/shard_map/ppermute | solution.py:328
  105.1 12.4 %all_to_all.20 = f32[32,16,128]{2,1,0:T(8,128)S(1)} all-to-all(f32[32,16,128]{2,1,0:T(8,128)S(1)} %broadcast_in_dim.14), channel_id=1, replica_groups=mesh['row'=32,'col'=4] {'row'}, dimensions={0} | all-to-all | bytes 524288 | tf_op jit(solution)/shard_map/all_to_all | solution.py:367
  117.5 3.2 %collective-permute-done.27.one_ref = f32[256,1024]{1,0:T(8,128)S(1)} collective-permute-done((f32[256,1024]{1,0:T(8,128)S(1)}, f32[256,1024]{1,0:T(8,128)S(1)}, u32[]{:S(2)}, u32[]{:S(2)}) %collective-permute-start.27) | collective-permute-done | bytes 1048608 | tf_op jit(solution)/shard_map/ppermute | solution.py:359
  122.7 2.1 collective-permute-start.30
  126.7 3.3 %collective-permute-start.31 = (f32[256,1024]{1,0:T(8,128)S(1)}, f32[256,1024]{1,0:T(8,128)S(1)}, u32[]{:S(2)}, u32[]{:S(2)}) collective-permute-start(f32[256,1024]{1,0:T(8,128)S(1)} %get-tuple-element.77.own_ref), channel_id=1, source_target_pairs={{0,3},{1,0},{2,1},{3,2},{4,5},{5,6},{6,7},{7,4},{8,11},{9,8},{10,9... | collective-permute-start | bytes 3145736 | tf_op jit(solution)/shard_map/ppermute | solution.py:359
  130.0 12.8 %all_to_all.21 = f32[32,8,128]{2,1,0:T(8,128)S(1)} all-to-all(f32[32,8,128]{2,1,0:T(8,128)S(1)} %broadcast_in_dim.15), channel_id=1, replica_groups=mesh['row'=32,'col'=4] {'row'}, dimensions={0} | all-to-all | bytes 262144 | tf_op jit(solution)/shard_map/all_to_all | solution.py:367
  144.8 2.6 %collective-permute-start.33 = (f32[256]{0:T(256)S(1)}, f32[256]{0:T(256)S(1)}, u32[]{:S(2)}, u32[]{:S(2)}) collective-permute-start(f32[256]{0:T(256)S(1)} %exponential_reduce_fusion.3), channel_id=1, source_target_pairs={{0,1},{1,2},{2,3},{3,0},{4,5},{5,6},{6,7},{7,4},{8,9},{9,10},{10,1... | collective-permute-start | bytes 3080 | tf_op jit(solution)/shard_map/ppermute | solution.py:328
  151.4 11.4 %all_to_all.22 = f32[32,8,128]{2,1,0:T(8,128)S(1)} all-to-all(f32[32,8,128]{2,1,0:T(8,128)S(1)} %broadcast_in_dim.16), channel_id=1, replica_groups=mesh['row'=32,'col'=4] {'row'}, dimensions={0} | all-to-all | bytes 262144 | tf_op jit(solution)/shard_map/all_to_all | solution.py:367
  162.7 4.6 %collective-permute-done.35.three_ref = f32[256,1024]{1,0:T(8,128)S(1)} collective-permute-done((f32[256,1024]{1,0:T(8,128)S(1)}, f32[256,1024]{1,0:T(8,128)S(1)}, u32[]{:S(2)}, u32[]{:S(2)}) %collective-permute-start.35) | collective-permute-done | bytes 1048608 | tf_op jit(solution)/shard_map/ppermute | solution.py:359
  174.9 3.9 %all-to-all-start.3 = ((f32[32,8,128]{2,1,0:T(8,128)}), f32[32,8,128]{2,1,0:T(8,128)S(1)}, u32[]{:S(2)}, u32[]{:S(2)}) async-start(f32[32,8,128]{2,1,0:T(8,128)} %broadcast_in_dim.19), calls=%async_computation.3 | async-start | bytes 262144 | tf_op jit(solution)/shard_map/all_to_all | solution.py:367
  178.9 7.6 %all-to-all-done.3 = f32[32,8,128]{2,1,0:T(8,128)S(1)} async-done(((f32[32,8,128]{2,1,0:T(8,128)}), f32[32,8,128]{2,1,0:T(8,128)S(1)}, u32[]{:S(2)}, u32[]{:S(2)}) %all-to-all-start.3) | async-done | bytes 131104 | tf_op jit(solution)/shard_map/all_to_all | solution.py:367
  189.1 2.5 %collective-permute-start.40 = (f32[1024]{0:T(1024)S(1)}, f32[1024]{0:T(1024)S(1)}, u32[]{:S(2)}, u32[]{:S(2)}) collective-permute-start(f32[1024]{0:T(1024)S(1)} %get-tuple-element.90), channel_id=1, source_target_pairs={{0,2},{1,3},{2,0},{3,1},{4,6},{5,7},{6,4},{7,5},{8,10},{9,11},{10,... | collective-permute-start | bytes 12296 | tf_op jit(solution)/shard_map/ppermute | solution.py:328
  192.0 2.3 %collective-permute-done.40 = f32[1024]{0:T(1024)S(1)} collective-permute-done((f32[1024]{0:T(1024)S(1)}, f32[1024]{0:T(1024)S(1)}, u32[]{:S(2)}, u32[]{:S(2)}) %collective-permute-start.40) | collective-permute-done | bytes 4128 | tf_op jit(solution)/shard_map/ppermute | solution.py:328
  196.5 11.6 %shard_map.54 = (f32[256,1024]{1,0:T(8,128)}, f32[256,128]{1,0:T(8,128)S(1)}) custom-call(s32[2]{0:T(128)S(1)} %pad_add_fusion.place_ref, f32[256,1]{1,0:T(8,128)S(1)} %copy.6.noise_ref, f32[4,1,1024]{2,1,0:T(1,128)S(1)} %broadcast_in_dim.20.data_pot_ref, f32[256,1024]{1,0:T(8,128)S(1)} %get-tuple-element.77.own_ref, ...), custom_call_target="tpu_custom_call" | custom-call | flops 6442450944 | bytes 20971520 | tf_op jit(solution)/shard_map/pallas_call | solution.py:307
  (152 shorter events, 61.2 us)
Async XLA Ops:
  7.2 79.3 %all-gather.5.cloned.1.call-start = ((), (), s32[]{:S(2)}) async-start(), calls=%async_computation.4 | async-start | bytes 8650752 | tf_op jit(solution)/shard_map/all_gather | solution.py:386
  8.9 186.4 %all-gather.7.cloned.1.call-start = ((), (), s32[]{:S(2)}) async-start(), calls=%async_computation.5 | async-start | bytes 17301504 | tf_op jit(solution)/shard_map/all_gather | solution.py:419
  10.0 7.4 %collective-permute-start = (f32[256,128]{1,0:T(8,128)S(1)}, f32[256,128]{1,0:T(8,128)S(1)}, u32[]{:S(2)}, u32[]{:S(2)}) collective-permute-start(f32[256,128]{1,0:T(8,128)S(1)} %get-tuple-element.49), channel_id=1, source_target_pairs={{0,8},{4,12},{8,16},{12,20},{16,24},{20,28},{24,0},{28,4},{32,40},... | collective-permute-start | bytes 393224 | tf_op jit(solution)/shard_map/ppermute | solution.py:336
  11.6 6.2 %collective-permute-start.2 = (f32[256,128]{1,0:T(8,128)S(1)}, f32[256,128]{1,0:T(8,128)S(1)}, u32[]{:S(2)}, u32[]{:S(2)}) collective-permute-start(f32[256,128]{1,0:T(8,128)S(1)} %get-tuple-element.49), channel_id=1, source_target_pairs={{0,24},{4,28},{8,0},{12,4},{16,8},{20,12},{24,16},{28,20},{32,56},... | collective-permute-start | bytes 393224 | tf_op jit(solution)/shard_map/ppermute | solution.py:336
  13.3 7.5 %collective-permute-start.4 = (f32[256,128]{1,0:T(8,128)S(1)}, f32[256,128]{1,0:T(8,128)S(1)}, u32[]{:S(2)}, u32[]{:S(2)}) collective-permute-start(f32[256,128]{1,0:T(8,128)S(1)} %get-tuple-element.54), channel_id=1, source_target_pairs={{0,32},{4,36},{8,40},{12,44},{16,48},{20,52},{24,56},{28,60},{32,6... | collective-permute-start | bytes 393224 | tf_op jit(solution)/shard_map/ppermute | solution.py:332
  15.3 6.6 %collective-permute-start.6 = (f32[256,128]{1,0:T(8,128)S(1)}, f32[256,128]{1,0:T(8,128)S(1)}, u32[]{:S(2)}, u32[]{:S(2)}) collective-permute-start(f32[256,128]{1,0:T(8,128)S(1)} %get-tuple-element.54), channel_id=1, source_target_pairs={{0,96},{4,100},{8,104},{12,108},{16,112},{20,116},{24,120},{28,124... | collective-permute-start | bytes 393224 | tf_op jit(solution)/shard_map/ppermute | solution.py:332
  17.4 6.8 %collective-permute-start.1 = (f32[128,128]{1,0:T(8,128)S(1)}, f32[128,128]{1,0:T(8,128)S(1)}, u32[]{:S(2)}, u32[]{:S(2)}) collective-permute-start(f32[128,128]{1,0:T(8,128)S(1)} %slice.84), channel_id=1, source_target_pairs={{0,8},{4,12},{8,16},{12,20},{16,24},{20,28},{24,0},{28,4},{32,40},... | collective-permute-start | bytes 196616 | tf_op jit(solution)/shard_map/ppermute | solution.py:336
  17.8 6.4 %collective-permute-start.3 = (f32[128,128]{1,0:T(8,128)S(1)}, f32[128,128]{1,0:T(8,128)S(1)}, u32[]{:S(2)}, u32[]{:S(2)}) collective-permute-start(f32[128,128]{1,0:T(8,128)S(1)} %slice.85), channel_id=1, source_target_pairs={{0,24},{4,28},{8,0},{12,4},{16,8},{20,12},{24,16},{28,20},{32,56},... | collective-permute-start | bytes 196616 | tf_op jit(solution)/shard_map/ppermute | solution.py:336
  20.8 5.5 %collective-permute-start.5 = (f32[128,128]{1,0:T(8,128)S(1)}, f32[128,128]{1,0:T(8,128)S(1)}, u32[]{:S(2)}, u32[]{:S(2)}) collective-permute-start(f32[128,128]{1,0:T(8,128)S(1)} %slice.86), channel_id=1, source_target_pairs={{0,32},{4,36},{8,40},{12,44},{16,48},{20,52},{24,56},{28,60},{32,6... | collective-permute-start | bytes 196616 | tf_op jit(solution)/shard_map/ppermute | solution.py:332
  21.9 5.5 %collective-permute-start.7 = (f32[128,128]{1,0:T(8,128)S(1)}, f32[128,128]{1,0:T(8,128)S(1)}, u32[]{:S(2)}, u32[]{:S(2)}) collective-permute-start(f32[128,128]{1,0:T(8,128)S(1)} %slice.87), channel_id=1, source_target_pairs={{0,96},{4,100},{8,104},{12,108},{16,112},{20,116},{24,120},{28,124... | collective-permute-start | bytes 196616 | tf_op jit(solution)/shard_map/ppermute | solution.py:332
  27.4 36.9 %collective-permute-start.8 = (f32[256,4096]{1,0:T(8,128)}, f32[256,4096]{1,0:T(8,128)}, u32[]{:S(2)}, u32[]{:S(2)}) collective-permute-start(f32[256,4096]{1,0:T(8,128)} %value_ref), channel_id=1, source_target_pairs={{0,4},{4,0},{8,12},{12,8},{16,20},{20,16},{24,28},{28,24},{32,36},... | collective-permute-start | bytes 12582920 | tf_op jit(solution)/shard_map/ppermute | solution.py:340
  28.5 8.9 %collective-permute-start.17 = (f32[256,128]{1,0:T(8,128)S(1)}, f32[256,128]{1,0:T(8,128)S(1)}, u32[]{:S(2)}, u32[]{:S(2)}) collective-permute-start(f32[256,128]{1,0:T(8,128)S(1)} %get-tuple-element.100), channel_id=1, source_target_pairs={{0,32},{4,36},{8,40},{12,44},{16,48},{20,52},{24,56},{28,60},{32,6... | collective-permute-start | bytes 393224 | tf_op jit(solution)/shard_map/ppermute | solution.py:332
  30.5 10.1 %collective-permute-start.18 = (f32[256,128]{1,0:T(8,128)S(1)}, f32[256,128]{1,0:T(8,128)S(1)}, u32[]{:S(2)}, u32[]{:S(2)}) collective-permute-start(f32[256,128]{1,0:T(8,128)S(1)} %get-tuple-element.99), channel_id=1, source_target_pairs={{0,64},{4,68},{8,72},{12,76},{16,80},{20,84},{24,88},{28,92},{32,9... | collective-permute-start | bytes 393224 | tf_op jit(solution)/shard_map/ppermute | solution.py:332
  32.3 9.1 %collective-permute-start.19 = (f32[256,128]{1,0:T(8,128)S(1)}, f32[256,128]{1,0:T(8,128)}, u32[]{:S(2)}, u32[]{:S(2)}) collective-permute-start(f32[256,128]{1,0:T(8,128)S(1)} %get-tuple-element.98), channel_id=1, source_target_pairs={{0,96},{4,100},{8,104},{12,108},{16,112},{20,116},{24,120},{28,124... | collective-permute-start | bytes 393224 | tf_op jit(solution)/shard_map/ppermute | solution.py:332
  34.5 22.4 %collective-permute-start.10 = (f32[4,256,128]{2,1,0:T(8,128)S(1)}, f32[4,256,128]{2,1,0:T(8,128)S(1)}, u32[]{:S(2)}, u32[]{:S(2)}) collective-permute-start(f32[4,256,128]{2,1,0:T(8,128)S(1)} %pad_maximum_fusion.refs_0_), channel_id=1, source_target_pairs={{0,96},{4,100},{8,104},{12,108},{16,112},{20,116},{24,120},{28,124... | collective-permute-start | bytes 1572872 | tf_op jit(solution)/shard_map/ppermute | solution.py:332
  37.4 18.2 %collective-permute-start.9 = (f32[4,256,128]{2,1,0:T(8,128)S(1)}, f32[4,256,128]{2,1,0:T(8,128)S(1)}, u32[]{:S(2)}, u32[]{:S(2)}) collective-permute-start(f32[4,256,128]{2,1,0:T(8,128)S(1)} %pad_maximum_fusion.refs_0_), channel_id=1, source_target_pairs={{0,32},{4,36},{8,40},{12,44},{16,48},{20,52},{24,56},{28,60},{32,6... | collective-permute-start | bytes 1572872 | tf_op jit(solution)/shard_map/ppermute | solution.py:332
  40.6 21.0 %collective-permute-start.11 = (f32[4,256,128]{2,1,0:T(8,128)S(1)}, f32[4,256,128]{2,1,0:T(8,128)S(1)}, u32[]{:S(2)}, u32[]{:S(2)}) collective-permute-start(f32[4,256,128]{2,1,0:T(8,128)S(1)} %pad_maximum_fusion.1.refs_3_), channel_id=1, source_target_pairs={{0,8},{4,12},{8,16},{12,20},{16,24},{20,28},{24,0},{28,4},{32,40},... | collective-permute-start | bytes 1572872 | tf_op jit(solution)/shard_map/ppermute | solution.py:336
  41.4 22.9 %collective-permute-start.12 = (f32[4,256,128]{2,1,0:T(8,128)S(1)}, f32[4,256,128]{2,1,0:T(8,128)S(1)}, u32[]{:S(2)}, u32[]{:S(2)}) collective-permute-start(f32[4,256,128]{2,1,0:T(8,128)S(1)} %pad_maximum_fusion.1.refs_3_), channel_id=1, source_target_pairs={{0,24},{4,28},{8,0},{12,4},{16,8},{20,12},{24,16},{28,20},{32,56},... | collective-permute-start | bytes 1572872 | tf_op jit(solution)/shard_map/ppermute | solution.py:336
  55.6 28.8 %collective-permute-start.20 = (f32[256,128]{1,0:T(8,128)}, f32[256,128]{1,0:T(8,128)S(1)}, u32[]{:S(2)}, u32[]{:S(2)}) collective-permute-start(f32[256,128]{1,0:T(8,128)} %get-tuple-element.96), channel_id=1, source_target_pairs={{0,1},{1,2},{2,3},{3,0},{4,5},{5,6},{6,7},{7,4},{8,9},{9,10},{10,1... | collective-permute-start | bytes 393224 | tf_op jit(solution)/shard_map/ppermute | solution.py:328
  56.9 19.6 %collective-permute-start.13 = (f32[2,256,128]{2,1,0:T(8,128)S(1)}, f32[2,256,128]{2,1,0:T(8,128)S(1)}, u32[]{:S(2)}, u32[]{:S(2)}) collective-permute-start(f32[2,256,128]{2,1,0:T(8,128)S(1)} %slice.88), channel_id=1, source_target_pairs={{0,32},{4,36},{8,40},{12,44},{16,48},{20,52},{24,56},{28,60},{32,6... | collective-permute-start | bytes 786440 | tf_op jit(solution)/shard_map/ppermute | solution.py:332
  61.6 17.6 %collective-permute-start.14 = (f32[2,256,128]{2,1,0:T(8,128)S(1)}, f32[2,256,128]{2,1,0:T(8,128)S(1)}, u32[]{:S(2)}, u32[]{:S(2)}) collective-permute-start(f32[2,256,128]{2,1,0:T(8,128)S(1)} %slice.89), channel_id=1, source_target_pairs={{0,96},{4,100},{8,104},{12,108},{16,112},{20,116},{24,120},{28,124... | collective-permute-start | bytes 786440 | tf_op jit(solution)/shard_map/ppermute | solution.py:332
  64.3 16.3 %collective-permute-start.15 = (f32[2,256,128]{2,1,0:T(8,128)S(1)}, f32[2,256,128]{2,1,0:T(8,128)S(1)}, u32[]{:S(2)}, u32[]{:S(2)}) collective-permute-start(f32[2,256,128]{2,1,0:T(8,128)S(1)} %slice.90), channel_id=1, source_target_pairs={{0,8},{4,12},{8,16},{12,20},{16,24},{20,28},{24,0},{28,4},{32,40},... | collective-permute-start | bytes 786440 | tf_op jit(solution)/shard_map/ppermute | solution.py:336
  64.3 16.3 %collective-permute-start.16 = (f32[2,256,128]{2,1,0:T(8,128)S(1)}, f32[2,256,128]{2,1,0:T(8,128)S(1)}, u32[]{:S(2)}, u32[]{:S(2)}) collective-permute-start(f32[2,256,128]{2,1,0:T(8,128)S(1)} %slice.91), channel_id=1, source_target_pairs={{0,24},{4,28},{8,0},{12,4},{16,8},{20,12},{24,16},{28,20},{32,56},... | collective-permute-start | bytes 786440 | tf_op jit(solution)/shard_map/ppermute | solution.py:336
  76.4 8.0 %collective-permute-start.21 = (f32[256,128]{1,0:T(8,128)S(1)}, f32[256,128]{1,0:T(8,128)S(1)}, u32[]{:S(2)}, u32[]{:S(2)}) collective-permute-start(f32[256,128]{1,0:T(8,128)S(1)} %get-tuple-element.95), channel_id=1, source_target_pairs={{0,2},{1,3},{2,0},{3,1},{4,6},{5,7},{6,4},{7,5},{8,10},{9,11},{10,... | collective-permute-start | bytes 393224 | tf_op jit(solution)/shard_map/ppermute | solution.py:328
  79.3 5.2 %collective-permute-start.22 = (f32[256,128]{1,0:T(8,128)S(1)}, f32[256,128]{1,0:T(8,128)S(1)}, u32[]{:S(2)}, u32[]{:S(2)}) collective-permute-start(f32[256,128]{1,0:T(8,128)S(1)} %get-tuple-element.94), channel_id=1, source_target_pairs={{0,3},{1,0},{2,1},{3,2},{4,7},{5,4},{6,5},{7,6},{8,11},{9,8},{10,9... | collective-permute-start | bytes 393224 | tf_op jit(solution)/shard_map/ppermute | solution.py:328
  104.5 16.3 %collective-permute-start.27 = (f32[256,1024]{1,0:T(8,128)S(1)}, f32[256,1024]{1,0:T(8,128)S(1)}, u32[]{:S(2)}, u32[]{:S(2)}) collective-permute-start(f32[256,1024]{1,0:T(8,128)S(1)} %get-tuple-element.77.own_ref), channel_id=1, source_target_pairs={{0,1},{1,2},{2,3},{3,0},{4,7},{5,4},{6,5},{7,6},{8,9},{9,10},{10,1... | collective-permute-start | bytes 3145736 | tf_op jit(solution)/shard_map/ppermute | solution.py:359
  121.2 5.2 %collective-permute-start.28 = (f32[256]{0:T(256)S(1)}, f32[256]{0:T(256)S(1)}, u32[]{:S(2)}, u32[]{:S(2)}) collective-permute-start(f32[256]{0:T(256)S(1)} %exponential_reduce_fusion.5), channel_id=1, source_target_pairs={{0,2},{1,3},{2,0},{3,1},{4,6},{5,7},{6,4},{7,5},{8,10},{9,11},{10,... | collective-permute-start | bytes 3080 | tf_op jit(solution)/shard_map/ppermute | solution.py:328
  126.7 16.1 %collective-permute-start.31 = (f32[256,1024]{1,0:T(8,128)S(1)}, f32[256,1024]{1,0:T(8,128)S(1)}, u32[]{:S(2)}, u32[]{:S(2)}) collective-permute-start(f32[256,1024]{1,0:T(8,128)S(1)} %get-tuple-element.77.own_ref), channel_id=1, source_target_pairs={{0,3},{1,0},{2,1},{3,2},{4,5},{5,6},{6,7},{7,4},{8,11},{9,8},{10,9... | collective-permute-start | bytes 3145736 | tf_op jit(solution)/shard_map/ppermute | solution.py:359
  143.2 5.2 %collective-permute-start.32 = (f32[256]{0:T(256)S(1)}, f32[256]{0:T(256)S(1)}, u32[]{:S(2)}, u32[]{:S(2)}) collective-permute-start(f32[256]{0:T(256)S(1)} %exponential_reduce_fusion.3), channel_id=1, source_target_pairs={{0,2},{1,3},{2,0},{3,1},{4,6},{5,7},{6,4},{7,5},{8,10},{9,11},{10,... | collective-permute-start | bytes 3080 | tf_op jit(solution)/shard_map/ppermute | solution.py:328
  151.3 16.1 %collective-permute-start.35 = (f32[256,1024]{1,0:T(8,128)S(1)}, f32[256,1024]{1,0:T(8,128)S(1)}, u32[]{:S(2)}, u32[]{:S(2)}) collective-permute-start(f32[256,1024]{1,0:T(8,128)S(1)} %collective-permute-done.27.one_ref), channel_id=1, source_target_pairs={{0,1},{1,2},{2,3},{3,0},{4,7},{5,4},{6,5},{7,6},{8,9},{9,10},{10,1... | collective-permute-start | bytes 3145736 | tf_op jit(solution)/shard_map/ppermute | solution.py:359
  168.7 5.2 %collective-permute-start.36 = (f32[256]{0:T(256)S(1)}, f32[256]{0:T(256)S(1)}, u32[]{:S(2)}, u32[]{:S(2)}) collective-permute-start(f32[256]{0:T(256)S(1)} %exponential_reduce_fusion.1), channel_id=1, source_target_pairs={{0,2},{1,3},{2,0},{3,1},{4,6},{5,7},{6,4},{7,5},{8,10},{9,11},{10,... | collective-permute-start | bytes 3080 | tf_op jit(solution)/shard_map/ppermute | solution.py:328
  174.9 11.7 %all-to-all-start.3 = ((f32[32,8,128]{2,1,0:T(8,128)}), f32[32,8,128]{2,1,0:T(8,128)S(1)}, u32[]{:S(2)}, u32[]{:S(2)}) async-start(f32[32,8,128]{2,1,0:T(8,128)} %broadcast_in_dim.19), calls=%async_computation.3 | async-start | bytes 262144 | tf_op jit(solution)/shard_map/all_to_all | solution.py:367
  (24 other events, 86.3 us)
Sparse Core Ops, SparseCore 0:
  10.3 68.7 all-gather.4
  86.6 71.0 all-gather.6
